TPU v7x, 512 devices: a whole 4x4x16 slice. The times are simulated.
512 devices in a mesh: ctx: 32 (over x, y, core), head: 16 (over z).
Axes of the slice: x: 4, y: 4, z: 16, core: 2. Of those that a mesh axis runs over, the one named last changes fastest.
Arguments:
- queries: bfloat16 [16384, 8192], P('ctx', 'head'), may hold values from -6 to 6
- key_rows: bfloat16 [16384, 8192], P('ctx', 'head'), may hold values from -6 to 6
- values: bfloat16 [16384, 8192], P('ctx', 'head'), may hold values from -7 to 7
- log_decay: float32 [64, 16384], P('head', 'ctx'), may hold values from -1.5 to 0, as said below
- norm_gain: float32 [8192], P('head'), may hold values from 0.25 to 1.75
- grad_normed: bfloat16 [16384, 8192], P('ctx', 'head'), may hold values from -6 to 6
Outputs:
- grad_queries: bfloat16 [16384, 8192], P('ctx', 'head')
- grad_keys: bfloat16 [16384, 8192], P('ctx', 'head')
- grad_values: bfloat16 [16384, 8192], P('ctx', 'head')
Inputs may be any that keep to these rules, and one draw needn't show every extreme that they name: `log_decay`: every entry is the logarithm of a decay factor, so it is below zero.
All inputs are finite; a program needn't handle non-finite values.
Results may differ from a plain program's by a relative error of at most 0.0063.
Values sent between devices are 32-bit elements; how exact they have to be, the bound alone decides.
No kernel may reach another device: no remote copies, remote signals or barrier semaphores. Data moves between devices by JAX's collectives and lax.ppermute only.
A program may use at most 64 MiB of HBM per device.

v0:
```python
import jax
import jax.numpy as jnp
from jax import lax
from jax.sharding import PartitionSpec as P

HEAD_COUNT = 64
HD = 128


EPSILON = 1e-05


def decay_table(log_rows):
    running = jnp.cumsum(log_rows, axis=1)
    length = log_rows.shape[1]
    token_positions = jnp.arange(length)
    causal = token_positions[:, None] >= token_positions[None, :]
    spread = running[:, :, None] - running[:, None, :]
    within = jnp.where(causal[None, :, :], jnp.exp(jnp.minimum(spread, 0.0)), 0.0)
    return (running, within)


def fold_states(shard_block, block_ends, block_starts, own_index, from_later):
    piece_count = shard_block.shape[0]
    sources = jnp.arange(piece_count, dtype=jnp.int32)
    own_end = lax.dynamic_index_in_dim(block_ends, own_index, 0, keepdims=False)
    own_start = lax.dynamic_index_in_dim(block_starts, own_index, 0, keepdims=False)
    if from_later:
        log_gap = block_starts - own_end[None, :]
        selected = sources > own_index
    else:
        log_gap = own_start[None, :] - block_ends
        selected = sources < own_index
    factor = jnp.where(selected[:, None], jnp.exp(jnp.minimum(log_gap, 0.0)), 0.0)
    return jnp.einsum("nh,nhde->hde", factor, shard_block, precision=lax.Precision.HIGHEST)


def on_device(queries, key_rows, values, log_decay, norm_gain, grad_normed):
    row_count = queries.shape[0]
    heads_here = log_decay.shape[0]
    head_width = queries.shape[1] // heads_here
    shape_three = (row_count, heads_here, head_width)
    query_block = queries.reshape(shape_three)
    key_block = key_rows.reshape(shape_three)
    value_block = values.reshape(shape_three)
    normed_block = grad_normed.reshape(shape_three)
    gain_block = norm_gain.reshape(heads_here, head_width)
    running, within = decay_table(log_decay)
    block_total = running[:, -1]
    head_weight = jnp.exp(running).T[:, :, None]
    tail_weight = jnp.exp(block_total[:, None] - running).T[:, :, None]
    scores = jnp.einsum("thd,jhd->htj", query_block, key_block, preferred_element_type=jnp.float32)
    masked = (scores * within).astype(jnp.bfloat16)
    scaled_keys = (key_block * tail_weight).astype(jnp.bfloat16)
    update = jnp.einsum(
        "jhd,jhe->hde", scaled_keys, value_block, preferred_element_type=jnp.float32
    )
    totals = lax.all_gather(block_total[None, :], "ctx", axis=0, tiled=True)
    block_ends = jnp.cumsum(totals, axis=0)
    block_starts = block_ends - totals
    own_index = lax.axis_index("ctx")
    state_in = fold_states(
        lax.all_gather(update[None], "ctx", axis=0, tiled=True),
        block_ends=block_ends,
        block_starts=block_starts,
        own_index=own_index,
        from_later=False,
    )
    state_low = state_in.astype(jnp.bfloat16)
    local_part = jnp.einsum("htj,jhe->the", masked, value_block, preferred_element_type=jnp.float32)
    carried = jnp.einsum("thd,hde->the", query_block, state_low, preferred_element_type=jnp.float32)
    output = local_part + head_weight * carried
    gained = normed_block * gain_block[None, :, :]
    square_sum, cross_sum = lax.psum(
        (jnp.sum(output * output, axis=(1, 2)), jnp.sum(output * gained, axis=(1, 2))), "head"
    )
    channels = HEAD_COUNT * HD
    inverse = lax.rsqrt(square_sum / channels + EPSILON)
    inner_mean = cross_sum / channels
    grad_output = (
        inverse[:, None, None] * gained
        - output * (inverse * inverse * inverse * inner_mean)[:, None, None]
    ).astype(jnp.bfloat16)
    pull_scores = jnp.einsum(
        "the,jhe->htj", grad_output, value_block, preferred_element_type=jnp.float32
    )
    pulled = (pull_scores * within).astype(jnp.bfloat16)
    scaled_queries = (query_block * head_weight).astype(jnp.bfloat16)
    back_update = jnp.einsum(
        "thd,the->hde", scaled_queries, grad_output, preferred_element_type=jnp.float32
    )
    state_out = fold_states(
        lax.all_gather(back_update[None], "ctx", axis=0, tiled=True),
        block_ends=block_ends,
        block_starts=block_starts,
        own_index=own_index,
        from_later=True,
    )
    out_low = state_out.astype(jnp.bfloat16)
    grad_query = jnp.einsum(
        "htj,jhd->thd", pulled, key_block, preferred_element_type=jnp.float32
    ) + head_weight * jnp.einsum(
        "the,hde->thd", grad_output, state_low, preferred_element_type=jnp.float32
    )
    grad_key = jnp.einsum(
        "htj,thd->jhd", pulled, query_block, preferred_element_type=jnp.float32
    ) + tail_weight * jnp.einsum(
        "jhe,hde->jhd", value_block, out_low, preferred_element_type=jnp.float32
    )
    grad_value = jnp.einsum(
        "htj,the->jhe", masked, grad_output, preferred_element_type=jnp.float32
    ) + tail_weight * jnp.einsum(
        "jhd,hde->jhe", key_block, out_low, preferred_element_type=jnp.float32
    )
    flat_width = heads_here * head_width
    return (
        grad_query.astype(jnp.bfloat16).reshape(row_count, flat_width),
        grad_key.astype(jnp.bfloat16).reshape(row_count, flat_width),
        grad_value.astype(jnp.bfloat16).reshape(row_count, flat_width),
    )


def solution(mesh):
    return jax.shard_map(
        on_device,
        mesh=mesh,
        in_specs=(
            P("ctx", "head"),
            P("ctx", "head"),
            P("ctx", "head"),
            P("head", "ctx"),
            P("head"),
            P("ctx", "head"),
        ),
        out_specs=(P("ctx", "head"), P("ctx", "head"), P("ctx", "head")),
        check_vma=False,
    )
```

profile of v0, /device:TPU:1, one launch (start us, length us, event | category | flops | bytes accessed | tf_op | source)
XLA Modules:
  0.0 217.7 jit_solution(4404040962756987342)
XLA Ops:
  7.2 0.0 copy-start
  7.2 0.0 all-gather.6.cloned.1.call-start
  7.2 0.8 reshape.88
  8.0 1.2 reduce-window.6
  9.2 0.2 slice_reduce_fusion
  9.4 0.2 reduce-window.9
  9.6 0.1 add_bitcast_fusion
  9.7 0.1 slice.13
  9.7 0.1 copy.88
  9.8 0.1 exponential_bitcast_fusion
  9.9 1.3 copy.50
  11.2 1.0 fusion.13
  12.2 0.0 all-gather.6.cloned.1.call-update
  12.2 0.0 all-gather.8.cloned.1.call-start
  12.3 1.3 dynamic-slice
  14.2 0.1 bitcast_dynamic-update-slice_fusion
  14.3 69.6 %all-reduce = f32[128]{0:T(128)S(1)} all-reduce(f32[128]{0:T(128)S(1)} %bitcast_dynamic-update-slice_fusion), channel_id=2, replica_groups=mesh['ctx'=32,'head'=16] {'ctx'}, use_global_device_ids=true, to_apply=%add | all-reduce | flops 128 | bytes 1024
  83.9 0.1 reshape.95
  84.0 0.1 reduce_window_sum.36
  84.1 0.1 select_bitcast_fusion
  84.2 0.1 select_bitcast_fusion.1
  84.3 0.1 copy.71
  84.3 1.3 copy.49
  85.6 0.2 copy.58
  85.8 0.1 iota_compare_fusion
  85.9 1.4 multiply_convert_fusion.1
  87.4 1.4 copy-done.1
  88.7 1.8 convolution_bitcast_fusion.3
  90.5 12.1 %fusion = f32[4,1,128,128]{3,1,2,0:T(1,128)S(1)} fusion(f32[32,4,1,1]{0,2,3,1:T(1,128)S(1)} %copy.71, f32[32,4,128,128]{3,2,1,0:T(8,128)} %bitcast.121), kind=kOutput, calls=%fused_computation.1 | convolution fusion | flops 25165824 | bytes 8651264 | tf_op jit(solution)/shard_map/nh,nhde->hde/dot_general | solution.py:35
  102.7 1.5 multiply_reduce_fusion.2
  104.2 24.3 %all-reduce.1 = (f32[512]{0:T(512)S(1)}, f32[512]{0:T(512)S(1)}) all-reduce(f32[512]{0:T(512)S(1)} %get-tuple-element.13, f32[512]{0:T(512)S(1)} %get-tuple-element.12), channel_id=1, replica_groups=mesh['ctx'=32,'head'=16] {'head'}, use_global_device_ids=true, to_apply=%region_6.7 | all-reduce | flops 1024 | bytes 8192 | tf_op jit(solution)/shard_map/psum | solution.py:74
  128.5 1.4 subtract_convert_fusion
  129.9 1.0 fusion.14
  130.9 0.0 all-gather.8.cloned.1.call-update
  131.0 1.4 multiply_convert_fusion
  132.4 1.3 copy-done.3
  133.7 2.0 convolution_bitcast_fusion.2
  135.7 2.2 fusion.10
  137.9 2.0 copy.66
  139.9 2.7 %convolution_bitcast_fusion.1 = f32[512,4,128]{0,2,1:T(8,128)} fusion(bf16[512,4,128]{0,2,1:T(8,128)(2,1)} %copy-done.5, bf16[4,512,512]{2,1,0:T(8,128)(2,1)S(1)} %copy-done.2), kind=kOutput, calls=%fused_computation.7 | convolution fusion | flops 268435456 | bytes 3670016 | tf_op jit(solution)/shard_map/htj,the->jhe/dot_general | solution.py:110
  142.6 0.4 convolution_bitcast_fusion
  143.1 59.0 %all-gather.8.cloned.1.call-done = f32[128,128,128]{2,1,0:T(8,128)} async-done(((f32[4,128,128]{2,1,0:T(8,128)}), f32[128,128,128]{2,1,0:T(8,128)}) %all-gather.8.cloned.1.call-update) | async-done | bytes 8388624 | tf_op jit(solution)/shard_map/all_gather | solution.py:93
  202.1 4.1 %multiply_reduce_fusion = bf16[4,128,128]{2,1,0:T(8,128)(2,1)S(1)} fusion(f32[4,32,128,128]{3,2,0,1:T(8,128)} %bitcast.122, f32[4,32]{0,1:T(8,128)S(1)} %get-tuple-element.16), kind=kLoop, calls=%fused_computation | loop fusion | flops 4128768 | bytes 8520192
  206.2 0.1 copy.85
  206.4 1.1 fusion.12
  207.5 2.0 copy.68
  209.5 0.4 fusion.11
  209.9 1.0 copy.67
  (28 shorter events, 0.1 us)
Async XLA Ops:
  7.2 4.0 %copy-start = (bf16[512,512]{1,0:T(8,128)(2,1)S(1)}, bf16[512,512]{1,0:T(8,128)(2,1)}, u32[]{:S(2)}) copy-start(bf16[512,512]{1,0:T(8,128)(2,1)} %param.8) | copy-start | bytes 1572868
  7.2 78.4 %copy-start.10 = (bf16[512,512]{1,0:T(8,128)(2,1)S(1)}, bf16[512,512]{1,0:T(8,128)(2,1)}, u32[]{:S(2)}) copy-start(bf16[512,512]{1,0:T(8,128)(2,1)} %param.11) | copy-start | bytes 1572868
  7.2 83.3 %all-gather.6.cloned.1.call-start = ((), (), s32[]{:S(2)}) async-start(), calls=%async_computation | async-start | bytes 8650752 | tf_op jit(solution)/shard_map/all_gather | solution.py:63
  11.2 76.2 %copy-start.6 = (bf16[512,512]{0,1:T(8,128)(2,1)}, bf16[512,512]{0,1:T(8,128)(2,1)S(1)}, u32[]{:S(2)}) copy-start(bf16[512,512]{0,1:T(8,128)(2,1)S(1)} %copy.50) | copy-start | bytes 1572868
  12.2 189.9 %all-gather.8.cloned.1.call-start = ((), (), s32[]{:S(2)}) async-start(), calls=%async_computation.1 | async-start | bytes 8650752 | tf_op jit(solution)/shard_map/all_gather | solution.py:93
  87.3 1.4 copy-start.1
  90.5 12.1 %copy-start.9 = (f32[512,4,128]{0,2,1:T(8,128)S(1)}, f32[512,4,128]{0,2,1:T(8,128)}, u32[]{:S(2)}) copy-start(f32[512,4,128]{0,2,1:T(8,128)} %convolution_bitcast_fusion.3) | copy-start | bytes 3145732
  90.5 12.1 %copy-start.11 = (f32[512]{0:T(512)S(1)}, f32[512]{0:T(512)}, u32[]{:S(2)}) copy-start(f32[512]{0:T(512)} %param.10) | copy-start | bytes 6148
  129.9 1.1 copy-start.5
  132.4 1.3 copy-start.3
  133.7 6.2 %copy-start.2 = (bf16[4,512,512]{2,1,0:T(8,128)(2,1)S(1)}, bf16[4,512,512]{2,1,0:T(8,128)(2,1)}, u32[]{:S(2)}) copy-start(bf16[4,512,512]{2,1,0:T(8,128)(2,1)} %copy-done.1) | copy-start | bytes 6291460
  139.9 2.7 %copy-start.4 = (bf16[4,512,512]{2,1,0:T(8,128)(2,1)S(1)}, bf16[4,512,512]{2,1,0:T(8,128)(2,1)}, u32[]{:S(2)}) copy-start(bf16[4,512,512]{2,1,0:T(8,128)(2,1)} %copy-done.3) | copy-start | bytes 6291460
  202.1 4.3 %copy-start.7 = (bf16[512,512]{0,1:T(8,128)(2,1)S(1)}, bf16[512,512]{0,1:T(8,128)(2,1)}, u32[]{:S(2)}) copy-start(bf16[512,512]{0,1:T(8,128)(2,1)} %copy-done.6) | copy-start | bytes 1572868
  202.1 4.3 %copy-start.8 = (f32[512,4,128]{0,2,1:T(8,128)S(1)}, f32[512,4,128]{0,2,1:T(8,128)}, u32[]{:S(2)}) copy-start(f32[512,4,128]{0,2,1:T(8,128)} %convolution_bitcast_fusion.1) | copy-start | bytes 3145732
Sparse Core Ops, SparseCore 0:
  12.3 74.1 all-gather.5
  131.1 70.9 all-gather.7
where the time goes:
time: 218 us
  blocking collectives  93.9 us (43%)
  waiting for transfers between devices  59.1 us (27%)
  matrix products  29 us (13%)
  between operations  14.9 us (7%)
  local copies, waits for them, and re-layouts  13.4 us (6%)
  other arithmetic  7.38 us (3%)
    unnamed x1, blocking collectives  69.6 us
    all_gather x1, waiting for transfers between devices, on_device(): lax.all_gather(back_update[None], 'ctx', axis=0, tiled=True)  59 us
    psum x1, blocking collectives, on_device(): lax.psum((jnp.sum(output * output, axis=(1, 2)), jnp.sum(output * gained,...  24.3 us
    dot_general x1, matrix products, fold_states(): jnp.einsum('nh,nhde->hde', factor, shard_block, precision=lax.Precision.H...  12.1 us
    unnamed x34, local copies, waits for them, and re-layouts  11.8 us
  transfers between devices with their start and end apart: 2, of which 1 were waited for; matrix products, arithmetic and copies ran while one was open for 8% of the time, Pallas kernels for 0%

commit v1 on v0

v1 whole, which is shorter than its diff:
```python
import jax
import jax.numpy as jnp
from jax import lax
from jax.experimental import pallas as pl
from jax.experimental.pallas import tpu as pltpu
from jax.sharding import PartitionSpec as P

HD = 128
EPSILON = 1e-05
F32 = jnp.float32
BF16 = jnp.bfloat16
VMEM_BYTES = 56 * 1024 * 1024


def dot(lhs, rhs, lhs_dim, rhs_dim):
    return lax.dot_general(
        lhs, rhs, (((lhs_dim,), (rhs_dim,)), ((), ())), preferred_element_type=F32
    )


def call(body, out_shapes, *operands, flops=0):
    moved = sum(a.size * a.dtype.itemsize for a in operands)
    moved += sum(s.size * s.dtype.itemsize for s in out_shapes)
    whole = pl.BlockSpec(memory_space=pltpu.VMEM)
    return pl.pallas_call(
        body,
        out_shape=out_shapes,
        in_specs=[whole] * len(operands),
        out_specs=[whole] * len(out_shapes),
        compiler_params=pltpu.CompilerParams(vmem_limit_bytes=VMEM_BYTES),
        cost_estimate=pl.CostEstimate(flops=flops, bytes_accessed=moved, transcendentals=0),
    )(*operands)


def like(shape, dtype=F32):
    return jax.ShapeDtypeStruct(shape, dtype)


def head_columns(head):
    return slice(head * HD, (head + 1) * HD)


def update_kernel(log_ref, key_ref, value_ref, send_ref, row_ref, column_ref):
    heads, length = log_ref.shape
    logs = jnp.concatenate([log_ref[...], jnp.zeros((8 - heads, length), F32)], axis=0)
    pieces = length // HD
    stacked = jnp.concatenate([logs[:, head_columns(i)] for i in range(pieces)], axis=0)
    before = lax.broadcasted_iota(jnp.int32, (HD, HD), 0)
    after = lax.broadcasted_iota(jnp.int32, (HD, HD), 1)
    upper = jnp.where(before <= after, 1.0, 0.0).astype(F32)
    sums = jnp.dot(
        stacked, upper, precision=lax.Precision.HIGHEST, preferred_element_type=F32
    )
    parts = []
    offset = jnp.zeros((8, 1), F32)
    for i in range(pieces):
        part = sums[i * 8 : (i + 1) * 8] + offset
        offset = part[:, HD - 1 : HD]
        parts.append(part)
    running = jnp.concatenate(parts, axis=1)
    row_ref[...] = running
    stack = jnp.concatenate(
        [running, jnp.exp(running), jnp.exp(offset - running), jnp.zeros((HD - 24, length), F32)],
        axis=0,
    )
    columns = stack.T
    column_ref[...] = columns
    targets, rows = send_ref.shape[0], send_ref.shape[1] - 8
    per_head = targets // heads
    for head in range(heads):
        tail = columns[:, 16 + head : 17 + head]
        scaled = (key_ref[:, head_columns(head)].astype(F32) * tail).astype(BF16)
        update = dot(scaled, value_ref[:, head_columns(head)], 0, 0)
        here = slice(head * per_head, (head + 1) * per_head)
        send_ref[here, :rows] = update.reshape(per_head, rows, HD)
        send_ref[here, rows:] = jnp.broadcast_to(
            offset[head : head + 1][None], (per_head, 8, HD)
        )


def forward_kernel(got_ref, send_ref, total_ref):
    blocks, rows = send_ref.shape[:2]
    totals = got_ref[:, rows : rows + 1, :]
    total_ref[...] = jnp.broadcast_to(totals, total_ref.shape)
    factors = jnp.exp(totals)
    state = jnp.zeros((rows, HD), F32)
    for block in range(blocks):
        send_ref[block] = state
        state = factors[block] * state + got_ref[block, :rows]


def backward_kernel(got_ref, total_ref, send_ref):
    blocks, rows = send_ref.shape[:2]
    factors = jnp.exp(total_ref[:, :1, :])
    state = jnp.zeros((rows, HD), F32)
    for block in reversed(range(blocks)):
        send_ref[block] = state
        state = factors[block] * state + got_ref[block]


def within_block(column, row, diagonal):
    spread = column - row
    if not diagonal:
        return jnp.exp(jnp.minimum(spread, 0.0))
    size = spread.shape[0]
    later = lax.broadcasted_iota(jnp.int32, (size, size), 0)
    earlier = lax.broadcasted_iota(jnp.int32, (size, size), 1)
    return jnp.where(later >= earlier, jnp.exp(jnp.minimum(spread, 0.0)), 0.0)


TILE = 256


def tiles(length):
    return [
        (slice(t, t + TILE), slice(j, j + TILE), t == j)
        for t in range(0, length, TILE)
        for j in range(0, t + TILE, TILE)
    ]


def local_kernel(query_ref, key_ref, value_ref, row_ref, column_ref, local_ref):
    length = query_ref.shape[0]
    for head in range(query_ref.shape[1] // HD):
        cols = head_columns(head)
        sums = {}
        for t, j, diagonal in tiles(length):
            within = within_block(
                column_ref[t, head : head + 1], row_ref[head : head + 1, j], diagonal
            )
            scores = dot(query_ref[t, cols], key_ref[j, cols], 1, 1)
            masked = (scores * within).astype(BF16)
            part = dot(masked, value_ref[j, cols], 1, 0)
            sums[t.start] = sums[t.start] + part if t.start in sums else part
        for start, value in sums.items():
            local_ref[start : start + TILE, cols] = value


def output_kernel(
    query_ref, local_ref, state_ref, column_ref, normed_ref, gain_ref, output_ref, send_ref
):
    length = query_ref.shape[0]
    squares = jnp.zeros((length, HD), F32)
    crosses = jnp.zeros((length, HD), F32)
    for head in range(query_ref.shape[1] // HD):
        cols = head_columns(head)
        carried = dot(query_ref[:, cols], state_ref[cols].astype(BF16), 1, 0)
        output = local_ref[:, cols] + column_ref[:, 8 + head : 9 + head] * carried
        output_ref[:, cols] = output
        gained = normed_ref[:, cols].astype(F32) * gain_ref[:, cols]
        squares = squares + output * output
        crosses = crosses + output * gained
    sums = []
    for total in (squares, crosses):
        for i in range(length // HD):
            sums.append(jnp.sum(total[head_columns(i)].T, axis=0, keepdims=True))
    packed = jnp.concatenate(sums, axis=0)
    send_ref[...] = jnp.broadcast_to(packed[None], send_ref.shape)


def grad_kernel(
    sums_ref, output_ref, normed_ref, gain_ref, query_ref, column_ref, grad_ref, send_ref
):
    length = query_ref.shape[0]
    heads = query_ref.shape[1] // HD
    pieces = length // HD
    channels = sums_ref.shape[0] * heads * HD
    sums = jnp.sum(sums_ref[...], axis=0)
    inverse = lax.rsqrt(sums[:pieces] / channels + EPSILON)
    inner = sums[pieces:] / channels
    scale = inverse * inverse * inverse * inner
    both = jnp.concatenate([inverse, scale, jnp.zeros((HD - 2 * pieces, HD), F32)], axis=0).T
    inverse = jnp.concatenate([both[:, i : i + 1] for i in range(pieces)], axis=0)
    scale = jnp.concatenate([both[:, pieces + i : pieces + i + 1] for i in range(pieces)], axis=0)
    targets, rows = send_ref.shape[:2]
    per_head = targets // heads
    for head in range(heads):
        cols = head_columns(head)
        gained = normed_ref[:, cols].astype(F32) * gain_ref[:, cols]
        grad = (inverse * gained - output_ref[:, cols] * scale).astype(BF16)
        grad_ref[:, cols] = grad
        scaled = (query_ref[:, cols].astype(F32) * column_ref[:, 8 + head : 9 + head]).astype(BF16)
        send_ref[head * per_head : (head + 1) * per_head] = dot(scaled, grad, 0, 0).reshape(
            per_head, rows, HD
        )


def pull_kernel(
    query_ref,
    key_ref,
    value_ref,
    grad_ref,
    state_ref,
    row_ref,
    column_ref,
    grad_query_ref,
    key_part_ref,
    value_part_ref,
):
    length = query_ref.shape[0]

    def add(sums, where, part):
        sums[where] = sums[where] + part if where in sums else part

    for head in range(query_ref.shape[1] // HD):
        cols = head_columns(head)
        query_sums, key_sums, value_sums = {}, {}, {}
        for t, j, diagonal in tiles(length):
            within = within_block(
                column_ref[t, head : head + 1], row_ref[head : head + 1, j], diagonal
            )
            query, key, value, grad = (
                query_ref[t, cols],
                key_ref[j, cols],
                value_ref[j, cols],
                grad_ref[t, cols],
            )
            pulled = (dot(grad, value, 1, 1) * within).astype(BF16)
            masked = (dot(query, key, 1, 1) * within).astype(BF16)
            add(query_sums, t.start, dot(pulled, key, 1, 0))
            add(key_sums, j.start, dot(pulled, query, 0, 0))
            add(value_sums, j.start, dot(masked, grad, 0, 0))
        low = state_ref[cols].astype(BF16)
        for start in range(0, length, TILE):
            here = slice(start, start + TILE)
            carried = dot(grad_ref[here, cols], low, 1, 1)
            grad_query_ref[here, cols] = (
                query_sums[start] + column_ref[here, 8 + head : 9 + head] * carried
            ).astype(BF16)
            key_part_ref[here, cols] = key_sums[start]
            value_part_ref[here, cols] = value_sums[start]


def finish_kernel(
    key_part_ref, value_part_ref, key_ref, value_ref, state_ref, column_ref, grad_key_ref, grad_value_ref
):
    for head in range(key_ref.shape[1] // HD):
        cols = head_columns(head)
        low = state_ref[cols].astype(BF16)
        tail = column_ref[:, 16 + head : 17 + head]
        grad_key_ref[:, cols] = (
            key_part_ref[:, cols] + tail * dot(value_ref[:, cols], low, 1, 1)
        ).astype(BF16)
        grad_value_ref[:, cols] = (
            value_part_ref[:, cols] + tail * dot(key_ref[:, cols], low, 1, 0)
        ).astype(BF16)


def on_device(blocks, groups, queries, key_rows, values, log_decay, norm_gain, grad_normed):
    length, width = queries.shape
    heads = log_decay.shape[0]
    rows = heads * HD // blocks
    gain = norm_gain.reshape(1, width)
    square = 2 * length * length * HD * heads
    narrow = 2 * length * HD * HD * heads

    def swap(array, axis):
        return lax.all_to_all(array, axis, 0, 0, tiled=True)

    first, row, column = call(
        update_kernel,
        [like((blocks, rows + 8, HD)), like((8, length)), like((length, HD))],
        log_decay,
        key_rows,
        values,
        flops=narrow,
    )
    got = swap(first, "ctx")
    (local,) = call(
        local_kernel, [like((length, width))], queries, key_rows, values, row, column, flops=2 * square
    )
    states, totals = call(
        forward_kernel, [like((blocks, rows, HD)), like((blocks, 8, HD))], got
    )
    state_in = swap(states, "ctx").reshape(heads * HD, HD)
    output, sums = call(
        output_kernel,
        [like((length, width)), like((groups, 2 * length // HD, HD))],
        queries,
        local,
        state_in,
        column,
        grad_normed,
        gain,
        flops=narrow,
    )
    sums = swap(sums, "head")
    grad, second = call(
        grad_kernel,
        [like((length, width), BF16), like((blocks, rows, HD))],
        sums,
        output,
        grad_normed,
        gain,
        queries,
        column,
        flops=narrow,
    )
    got = swap(second, "ctx")
    grad_query, key_part, value_part = call(
        pull_kernel,
        [like((length, width), BF16), like((length, width)), like((length, width))],
        queries,
        key_rows,
        values,
        grad,
        state_in,
        row,
        column,
        flops=5 * square,
    )
    (states,) = call(backward_kernel, [like((blocks, rows, HD))], got, totals)
    state_out = swap(states, "ctx").reshape(heads * HD, HD)
    grad_key, grad_value = call(
        finish_kernel,
        [like((length, width), BF16), like((length, width), BF16)],
        key_part,
        value_part,
        key_rows,
        values,
        state_out,
        column,
        flops=2 * narrow,
    )
    return grad_query, grad_key, grad_value


def solution(mesh):
    blocks, groups = mesh.shape["ctx"], mesh.shape["head"]

    def run(*arrays):
        return on_device(blocks, groups, *arrays)

    return jax.shard_map(
        run,
        mesh=mesh,
        in_specs=(
            P("ctx", "head"),
            P("ctx", "head"),
            P("ctx", "head"),
            P("head", "ctx"),
            P("head"),
            P("ctx", "head"),
        ),
        out_specs=(P("ctx", "head"), P("ctx", "head"), P("ctx", "head")),
        check_vma=False,
    )
```

time: 218 us -> 106 us (0.49)
  waiting for transfers between devices: 59.1 us -> 7.35 us
  blocking collectives: 93.9 us -> 60.9 us
  matrix products: 29 us -> 0 us
  Pallas kernels: 0 us -> 27.4 us
  between operations: 14.9 us -> 0.65 us
  local copies, waits for them, and re-layouts: 13.4 us -> 1.4 us
  other arithmetic: 7.38 us -> 0 us
  starting transfers between devices: 0.08 us -> 7.36 us
    unnamed x1 -> x0, blocking collectives: 69.6 us -> none
    all_to_all x0 -> x3, blocking collectives: none -> 60.9 us  [swap(): return lax.all_to_all(array, axis, 0, 0, tiled=True)]
    all_gather x2 -> x0, waiting for transfers between devices: 59 us -> none  [the longest x1 59 us: on_device(): lax.all_gather(back_update[None], 'ctx', axis=0, tiled=True)]
    dot_general x13 -> x0, matrix products: 29 us -> none  [the longest x1 12.1 us: fold_states(): jnp.einsum('nh,nhde->hde', factor, shard_block, precision=lax.Precision.H...]
    pallas_call x0 -> x8, Pallas kernels: none -> 27.4 us  [call(): pl.pallas_call(body, out_shape=out_shapes, in_specs=[whole] * len(operand...]
    psum x1 -> x0, blocking collectives: 24.3 us -> none  [on_device(): lax.psum((jnp.sum(output * output, axis=(1, 2)), jnp.sum(output * gained,...]
    unnamed x34 -> x4, local copies, waits for them, and re-layouts: 11.8 us -> 1.4 us
    all_to_all x0 -> x2, starting transfers between devices: none -> 7.36 us  [swap(): return lax.all_to_all(array, axis, 0, 0, tiled=True)]
  transfers between devices with their start and end apart: 2 -> 2, of which waited for: 1 -> 2; matrix products, arithmetic and copies ran while one was open for 8% -> 0% of each run, Pallas kernels for 0% -> 10%
where the time goes in v1:
time: 106 us; the launch traced here: 105 us
  blocking collectives  60.9 us (57%)
  Pallas kernels  27.4 us (26%)
  starting transfers between devices  7.36 us (7%)
  waiting for transfers between devices  7.35 us (7%)
  local copies, waits for them, and re-layouts  1.4 us (1%)
    all_to_all x3, blocking collectives, swap(): return lax.all_to_all(array, axis, 0, 0, tiled=True)  60.9 us
    pallas_call x8, Pallas kernels, call(): pl.pallas_call(body, out_shape=out_shapes, in_specs=[whole] * len(operand...  27.4 us
    all_to_all x2, starting transfers between devices, swap(): return lax.all_to_all(array, axis, 0, 0, tiled=True)  7.36 us
    all_to_all x2, waiting for transfers between devices, swap(): return lax.all_to_all(array, axis, 0, 0, tiled=True)  7.35 us
  transfers between devices with their start and end apart: 2, of which 2 were waited for; matrix products, arithmetic and copies ran while one was open for 0% of the time, Pallas kernels for 10%

profile of v1, /device:TPU:1, one launch (start us, length us, event | category | flops | bytes accessed | tf_op | source)
XLA Modules:
  0.0 105.0 jit_solution(2964031930194398165)
XLA Ops:
  0.6 3.2 %shard_map.85 = (f32[32,24,128]{2,1,0:T(8,128)}, f32[8,512]{1,0:T(8,128)}, f32[512,128]{1,0:T(8,128)}) custom-call(f32[4,512]{1,0:T(4,128)} %log_ref.1, bf16[512,512]{1,0:T(8,128)(2,1)} %key_ref.7, bf16[512,512]{1,0:T(8,128)(2,1)} %value_ref.7), custom_call_target="tpu_custom_call" | custom-call | flops 67108864 | bytes 1728512 | tf_op jit(solution)/shard_map/pallas_call | solution.py:25
  3.9 21.5 %all_to_all.25.got_ref = f32[32,24,128]{2,1,0:T(8,128)} all-to-all(f32[32,24,128]{2,1,0:T(8,128)} %get-tuple-element.19), channel_id=1, replica_groups=mesh['ctx'=32,'head'=16] {'ctx'}, dimensions={0} | all-to-all | bytes 786432 | tf_op jit(solution)/shard_map/all_to_all | solution.py:258
  25.4 1.8 %shard_map.87 = (f32[32,16,128]{2,1,0:T(8,128)}, f32[32,8,128]{2,1,0:T(8,128)}) custom-call(f32[32,24,128]{2,1,0:T(8,128)} %all_to_all.25.got_ref), custom_call_target="tpu_custom_call" | custom-call | bytes 786432 | tf_op jit(solution)/shard_map/pallas_call | solution.py:25
  27.2 3.7 %all-to-all-start.1 = ((f32[32,16,128]{2,1,0:T(8,128)}), f32[32,16,128]{2,1,0:T(8,128)S(1)}, u32[]{:S(2)}, u32[]{:S(2)}) async-start(f32[32,16,128]{2,1,0:T(8,128)} %get-tuple-element.20), calls=%async_computation.1 | async-start | bytes 524288 | tf_op jit(solution)/shard_map/all_to_all | solution.py:258
  30.8 4.0 %shard_map.86.local_ref = f32[512,512]{1,0:T(8,128)} custom-call(bf16[512,512]{1,0:T(8,128)(2,1)} %query_ref.7, bf16[512,512]{1,0:T(8,128)(2,1)} %key_ref.7, bf16[512,512]{1,0:T(8,128)(2,1)} %value_ref.7, f32[8,512]{1,0:T(8,128)} %get-tuple-element.17.row_ref, f32[512,128]{1,0:T(8,128)} %get-tuple-element.18.column_ref), custom_call_target="tpu_custom_call" | custom-call | flops 536870912 | bytes 2899968 | tf_op jit(solution)/shard_map/pallas_call | solution.py:25
  34.9 4.8 %all-to-all-done.1 = f32[32,16,128]{2,1,0:T(8,128)S(1)} async-done(((f32[32,16,128]{2,1,0:T(8,128)}), f32[32,16,128]{2,1,0:T(8,128)S(1)}, u32[]{:S(2)}, u32[]{:S(2)}) %all-to-all-start.1) | async-done | bytes 262176 | tf_op jit(solution)/shard_map/all_to_all | solution.py:258
  39.7 0.0 copy-start.1
  39.7 0.7 copy-done.1
  40.4 3.1 %shard_map.88 = (f32[512,512]{1,0:T(8,128)}, f32[16,8,128]{2,1,0:T(8,128)}) custom-call(bf16[512,512]{1,0:T(8,128)(2,1)} %query_ref.7, f32[512,512]{1,0:T(8,128)} %shard_map.86.local_ref, f32[512,128]{1,0:T(8,128)} %bitcast.4, f32[512,128]{1,0:T(8,128)} %get-tuple-element.18.column_ref, bf16[512,512]{1,0:T(8,128)(2,1)} %normed_ref.3, f32[1,512]{1,0:T(1,128)} %bitcast.6), custom_call_target="tpu_custom_call" | custom-call | flops 67108864 | bytes 3737600 | tf_op jit(solution)/shard_map/pallas_call | solution.py:25
  43.5 24.1 %all_to_all.26.sums_ref = f32[16,8,128]{2,1,0:T(8,128)} all-to-all(f32[16,8,128]{2,1,0:T(8,128)} %get-tuple-element.21), channel_id=1, replica_groups=mesh['ctx'=32,'head'=16] {'head'}, dimensions={0} | all-to-all | bytes 131072 | tf_op jit(solution)/shard_map/all_to_all | solution.py:258
  67.6 3.5 %shard_map.89 = (bf16[512,512]{1,0:T(8,128)(2,1)}, f32[32,16,128]{2,1,0:T(8,128)}) custom-call(f32[16,8,128]{2,1,0:T(8,128)} %all_to_all.26.sums_ref, f32[512,512]{1,0:T(8,128)} %get-tuple-element.22.output_ref, bf16[512,512]{1,0:T(8,128)(2,1)} %normed_ref.3, f32[1,512]{1,0:T(1,128)} %bitcast.7, bf16[512,512]{1,0:T(8,128)(2,1)} %query_ref.7, ...), custom_call_target="tpu_custom_call" | custom-call | flops 67108864 | bytes 3213312 | tf_op jit(solution)/shard_map/pallas_call | solution.py:25
  71.1 15.3 %all_to_all.27.got_ref = f32[32,16,128]{2,1,0:T(8,128)} all-to-all(f32[32,16,128]{2,1,0:T(8,128)} %get-tuple-element.27), channel_id=1, replica_groups=mesh['ctx'=32,'head'=16] {'ctx'}, dimensions={0} | all-to-all | bytes 524288 | tf_op jit(solution)/shard_map/all_to_all | solution.py:258
  86.4 1.8 %shard_map.91 = f32[32,16,128]{2,1,0:T(8,128)} custom-call(f32[32,16,128]{2,1,0:T(8,128)} %all_to_all.27.got_ref, f32[32,8,128]{2,1,0:T(8,128)} %get-tuple-element.28.total_ref), custom_call_target="tpu_custom_call" | custom-call | bytes 655360 | tf_op jit(solution)/shard_map/pallas_call | solution.py:25
  88.1 3.7 %all-to-all-start.4 = ((f32[32,16,128]{2,1,0:T(8,128)}), f32[32,16,128]{2,1,0:T(8,128)S(1)}, u32[]{:S(2)}, u32[]{:S(2)}) async-start(f32[32,16,128]{2,1,0:T(8,128)} %shard_map.91), calls=%async_computation.4 | async-start | bytes 524288 | tf_op jit(solution)/shard_map/all_to_all | solution.py:258
  91.8 6.6 %shard_map.90 = (bf16[512,512]{1,0:T(8,128)(2,1)}, f32[512,512]{1,0:T(8,128)}, f32[512,512]{1,0:T(8,128)}) custom-call(bf16[512,512]{1,0:T(8,128)(2,1)} %query_ref.7, bf16[512,512]{1,0:T(8,128)(2,1)} %key_ref.7, bf16[512,512]{1,0:T(8,128)(2,1)} %value_ref.7, bf16[512,512]{1,0:T(8,128)(2,1)} %get-tuple-element.23.grad_ref, f32[512,128]{1,0:T(8,128)} %bitcast.5, ...), custom_call_target="tpu_custom_call" | custom-call | flops 1342177280 | bytes 5259264 | tf_op jit(solution)/shard_map/pallas_call | solution.py:25
  98.4 2.5 %all-to-all-done.4 = f32[32,16,128]{2,1,0:T(8,128)S(1)} async-done(((f32[32,16,128]{2,1,0:T(8,128)}), f32[32,16,128]{2,1,0:T(8,128)S(1)}, u32[]{:S(2)}, u32[]{:S(2)}) %all-to-all-start.4) | async-done | bytes 262176 | tf_op jit(solution)/shard_map/all_to_all | solution.py:258
  100.9 0.0 copy-start
  100.9 0.7 copy-done
  101.6 3.4 %shard_map.92 = (bf16[512,512]{1,0:T(8,128)(2,1)}, bf16[512,512]{1,0:T(8,128)(2,1)}) custom-call(f32[512,512]{1,0:T(8,128)} %get-tuple-element.25.key_part_ref, f32[512,512]{1,0:T(8,128)} %get-tuple-element.26.value_part_ref, bf16[512,512]{1,0:T(8,128)(2,1)} %key_ref.7, bf16[512,512]{1,0:T(8,128)(2,1)} %value_ref.7, f32[512,128]{1,0:T(8,128)} %bitcast.3, ...), custom_call_target="tpu_custom_call" | custom-call | flops 134217728 | bytes 4718592 | tf_op jit(solution)/shard_map/pallas_call | solution.py:25
Async XLA Ops:
  27.2 12.5 %all-to-all-start.1 = ((f32[32,16,128]{2,1,0:T(8,128)}), f32[32,16,128]{2,1,0:T(8,128)S(1)}, u32[]{:S(2)}, u32[]{:S(2)}) async-start(f32[32,16,128]{2,1,0:T(8,128)} %get-tuple-element.20), calls=%async_computation.1 | async-start | bytes 524288 | tf_op jit(solution)/shard_map/all_to_all | solution.py:258
  39.7 0.7 copy-start.1
  88.1 12.8 %all-to-all-start.4 = ((f32[32,16,128]{2,1,0:T(8,128)}), f32[32,16,128]{2,1,0:T(8,128)S(1)}, u32[]{:S(2)}, u32[]{:S(2)}) async-start(f32[32,16,128]{2,1,0:T(8,128)} %shard_map.91), calls=%async_computation.4 | async-start | bytes 524288 | tf_op jit(solution)/shard_map/all_to_all | solution.py:258
  100.9 0.7 copy-start

commit v2 on v1

--- a/solution.py
+++ b/solution.py
@@ -9,7 +9,7 @@
 EPSILON = 1e-05
 F32 = jnp.float32
 BF16 = jnp.bfloat16
-VMEM_BYTES = 56 * 1024 * 1024
+VMEM_BYTES = 16 * 1024 * 1024
 
 
 def dot(lhs, rhs, lhs_dim, rhs_dim):
@@ -18,15 +18,28 @@
     )
 
 
-def call(body, out_shapes, *operands, flops=0):
+def call(body, out_shapes, *operands, flops=0, places_in={}, places_out={}, scratch=()):
     moved = sum(a.size * a.dtype.itemsize for a in operands)
     moved += sum(s.size * s.dtype.itemsize for s in out_shapes)
-    whole = pl.BlockSpec(memory_space=pltpu.VMEM)
+
+    def specs(count, outside):
+        return [
+            pl.BlockSpec(memory_space=outside.get(i, pltpu.VMEM)) for i in range(count)
+        ]
+
+    operands = [
+        pltpu.with_memory_space_constraint(a, places_in[i]) if i in places_in else a
+        for i, a in enumerate(operands)
+    ]
     return pl.pallas_call(
         body,
-        out_shape=out_shapes,
-        in_specs=[whole] * len(operands),
-        out_specs=[whole] * len(out_shapes),
+        out_shape=[
+            places_out[i](s.shape, s.dtype) if i in places_out else s
+            for i, s in enumerate(out_shapes)
+        ],
+        in_specs=specs(len(operands), places_in),
+        out_specs=specs(len(out_shapes), places_out),
+        scratch_shapes=scratch,
         compiler_params=pltpu.CompilerParams(vmem_limit_bytes=VMEM_BYTES),
         cost_estimate=pl.CostEstimate(flops=flops, bytes_accessed=moved, transcendentals=0),
     )(*operands)
@@ -40,17 +53,61 @@
     return slice(head * HD, (head + 1) * HD)
 
 
-def update_kernel(log_ref, key_ref, value_ref, send_ref, row_ref, column_ref):
+def turn(rows):
+    return jnp.concatenate([rows, jnp.zeros((HD - 8, rows.shape[1]), F32)], axis=0).T
+
+
+def tail_rows(row_ref):
+    running = row_ref[...]
+    return jnp.exp(running[:, running.shape[1] - 1 :] - running)
+
+
+def load_columns(sources, buffers, semaphores):
+    copies = []
+    for which, (source, buffer) in enumerate(zip(sources, buffers)):
+        copies.append([])
+        for head in range(source.shape[1] // HD):
+            cols = head_columns(head)
+            copy = pltpu.make_async_copy(
+                source.at[:, cols], buffer.at[:, cols], semaphores.at[which, head]
+            )
+            copies[which].append(copy)
+    for head in zip(*copies):
+        for copy in head:
+            copy.start()
+    return copies
+
+
+def update_kernel(
+    log_in,
+    key_in,
+    value_in,
+    send_ref,
+    row_ref,
+    log_ref,
+    log_semaphore,
+    key_ref,
+    value_ref,
+    semaphores,
+):
+    load_logs = pltpu.make_async_copy(log_in, log_ref, log_semaphore)
+    load_logs.start()
+    loads = load_columns((key_in, value_in), (key_ref, value_ref), semaphores)
     heads, length = log_ref.shape
+    load_logs.wait()
     logs = jnp.concatenate([log_ref[...], jnp.zeros((8 - heads, length), F32)], axis=0)
     pieces = length // HD
     stacked = jnp.concatenate([logs[:, head_columns(i)] for i in range(pieces)], axis=0)
+    high = stacked.astype(BF16)
+    rest = stacked - high.astype(F32)
+    middle = rest.astype(BF16)
+    low = (rest - middle.astype(F32)).astype(BF16)
     before = lax.broadcasted_iota(jnp.int32, (HD, HD), 0)
     after = lax.broadcasted_iota(jnp.int32, (HD, HD), 1)
-    upper = jnp.where(before <= after, 1.0, 0.0).astype(F32)
-    sums = jnp.dot(
-        stacked, upper, precision=lax.Precision.HIGHEST, preferred_element_type=F32
-    )
+    upper = jnp.where(before <= after, 1.0, 0.0).astype(BF16)
+    three = dot(jnp.concatenate([high, middle, low], axis=0), upper, 1, 0)
+    count = 8 * pieces
+    sums = (three[2 * count :] + three[count : 2 * count]) + three[:count]
     parts = []
     offset = jnp.zeros((8, 1), F32)
     for i in range(pieces):
@@ -59,23 +116,22 @@
         parts.append(part)
     running = jnp.concatenate(parts, axis=1)
     row_ref[...] = running
-    stack = jnp.concatenate(
-        [running, jnp.exp(running), jnp.exp(offset - running), jnp.zeros((HD - 24, length), F32)],
-        axis=0,
-    )
-    columns = stack.T
-    column_ref[...] = columns
+    tail = jnp.exp(offset - running)
     targets, rows = send_ref.shape[0], send_ref.shape[1] - 8
     per_head = targets // heads
     for head in range(heads):
-        tail = columns[:, 16 + head : 17 + head]
-        scaled = (key_ref[:, head_columns(head)].astype(F32) * tail).astype(BF16)
-        update = dot(scaled, value_ref[:, head_columns(head)], 0, 0)
         here = slice(head * per_head, (head + 1) * per_head)
-        send_ref[here, :rows] = update.reshape(per_head, rows, HD)
         send_ref[here, rows:] = jnp.broadcast_to(
             offset[head : head + 1][None], (per_head, 8, HD)
         )
+    for head in range(heads):
+        for load in loads:
+            load[head].wait()
+        turned = key_ref[:, head_columns(head)].T.astype(F32)
+        scaled = (turned * tail[head : head + 1]).astype(BF16)
+        update = dot(scaled, value_ref[:, head_columns(head)], 1, 0)
+        here = slice(head * per_head, (head + 1) * per_head)
+        send_ref[here, :rows] = update.reshape(per_head, rows, HD)
 
 
 def forward_kernel(got_ref, send_ref, total_ref):
@@ -119,9 +175,32 @@
     ]
 
 
-def local_kernel(query_ref, key_ref, value_ref, row_ref, column_ref, local_ref):
+def local_kernel(
+    query_in,
+    key_in,
+    value_in,
+    row_ref,
+    gain_in,
+    local_ref,
+    column_ref,
+    gain_ref,
+    query_ref,
+    key_ref,
+    value_ref,
+    semaphores,
+):
     length = query_ref.shape[0]
+    loads = load_columns(
+        (query_in, key_in, value_in), (query_ref, key_ref, value_ref), semaphores
+    )
+    gain_ref[...] = jnp.broadcast_to(gain_in[...], gain_ref.shape)
+    running = row_ref[...]
+    column_ref[...] = jnp.concatenate(
+        [running, jnp.exp(running), jnp.zeros((HD - 16, length), F32)], axis=0
+    ).T
     for head in range(query_ref.shape[1] // HD):
+        for load in loads:
+            load[head].wait()
         cols = head_columns(head)
         sums = {}
         for t, j, diagonal in tiles(length):
@@ -137,17 +216,18 @@
 
 
 def output_kernel(
-    query_ref, local_ref, state_ref, column_ref, normed_ref, gain_ref, output_ref, send_ref
+    query_ref, local_ref, state_ref, column_ref, normed_ref, gain_ref, output_ref, send_ref, low_ref
 ):
     length = query_ref.shape[0]
+    low_ref[...] = state_ref[...].reshape(low_ref.shape).astype(BF16)
     squares = jnp.zeros((length, HD), F32)
     crosses = jnp.zeros((length, HD), F32)
     for head in range(query_ref.shape[1] // HD):
         cols = head_columns(head)
-        carried = dot(query_ref[:, cols], state_ref[cols].astype(BF16), 1, 0)
+        carried = dot(query_ref[:, cols], low_ref[cols], 1, 0)
         output = local_ref[:, cols] + column_ref[:, 8 + head : 9 + head] * carried
         output_ref[:, cols] = output
-        gained = normed_ref[:, cols].astype(F32) * gain_ref[:, cols]
+        gained = normed_ref[:, cols].astype(F32) * gain_ref[:1, cols]
         squares = squares + output * output
         crosses = crosses + output * gained
     sums = []
@@ -176,7 +256,7 @@
     per_head = targets // heads
     for head in range(heads):
         cols = head_columns(head)
-        gained = normed_ref[:, cols].astype(F32) * gain_ref[:, cols]
+        gained = normed_ref[:, cols].astype(F32) * gain_ref[:1, cols]
         grad = (inverse * gained - output_ref[:, cols] * scale).astype(BF16)
         grad_ref[:, cols] = grad
         scaled = (query_ref[:, cols].astype(F32) * column_ref[:, 8 + head : 9 + head]).astype(BF16)
@@ -185,65 +265,101 @@
         )
 
 
+def add(sums, where, part):
+    sums[where] = sums[where] + part if where in sums else part
+
+
 def pull_kernel(
+    query_in,
+    key_in,
+    value_in,
+    grad_ref,
+    low_ref,
+    row_ref,
+    grad_query_out,
+    key_part_ref,
+    value_part_ref,
     query_ref,
     key_ref,
     value_ref,
-    grad_ref,
-    state_ref,
-    row_ref,
-    column_ref,
+    semaphores,
     grad_query_ref,
-    key_part_ref,
-    value_part_ref,
+    store_semaphores,
 ):
     length = query_ref.shape[0]
-
-    def add(sums, where, part):
-        sums[where] = sums[where] + part if where in sums else part
-
+    loads = load_columns(
+        (query_in, key_in, value_in), (query_ref, key_ref, value_ref), semaphores
+    )
+    stores = []
+    columns, grown = turn(row_ref[...]), turn(jnp.exp(row_ref[...]))
     for head in range(query_ref.shape[1] // HD):
+        for load in loads:
+            load[head].wait()
         cols = head_columns(head)
         query_sums, key_sums, value_sums = {}, {}, {}
         for t, j, diagonal in tiles(length):
             within = within_block(
-                column_ref[t, head : head + 1], row_ref[head : head + 1, j], diagonal
+                columns[t, head : head + 1], row_ref[head : head + 1, j], diagonal
             )
-            query, key, value, grad = (
-                query_ref[t, cols],
-                key_ref[j, cols],
-                value_ref[j, cols],
-                grad_ref[t, cols],
-            )
-            pulled = (dot(grad, value, 1, 1) * within).astype(BF16)
+            query, key, grad = query_ref[t, cols], key_ref[j, cols], grad_ref[t, cols]
+            pulled = (dot(grad, value_ref[j, cols], 1, 1) * within).astype(BF16)
             masked = (dot(query, key, 1, 1) * within).astype(BF16)
             add(query_sums, t.start, dot(pulled, key, 1, 0))
             add(key_sums, j.start, dot(pulled, query, 0, 0))
             add(value_sums, j.start, dot(masked, grad, 0, 0))
-        low = state_ref[cols].astype(BF16)
         for start in range(0, length, TILE):
             here = slice(start, start + TILE)
-            carried = dot(grad_ref[here, cols], low, 1, 1)
+            carried = dot(grad_ref[here, cols], low_ref[cols], 1, 1)
             grad_query_ref[here, cols] = (
-                query_sums[start] + column_ref[here, 8 + head : 9 + head] * carried
+                query_sums[start] + grown[here, head : head + 1] * carried
             ).astype(BF16)
             key_part_ref[here, cols] = key_sums[start]
             value_part_ref[here, cols] = value_sums[start]
+        stores.append(
+            pltpu.make_async_copy(
+                grad_query_ref.at[:, cols], grad_query_out.at[:, cols], store_semaphores.at[head]
+            )
+        )
+        stores[-1].start()
+    for store in stores:
+        store.wait()
 
 
 def finish_kernel(
-    key_part_ref, value_part_ref, key_ref, value_ref, state_ref, column_ref, grad_key_ref, grad_value_ref
-):
+    key_part_ref,
+    value_part_ref,
+    key_ref,
+    value_ref,
+    state_ref,
+    row_ref,
+    grad_key_out,
+    grad_value_out,
+    grad_key_ref,
+    grad_value_ref,
+    semaphores,
+):
+    low = state_ref[...].reshape(-1, HD).astype(BF16)
+    stores = []
+    tails = turn(tail_rows(row_ref))
     for head in range(key_ref.shape[1] // HD):
         cols = head_columns(head)
-        low = state_ref[cols].astype(BF16)
-        tail = column_ref[:, 16 + head : 17 + head]
+        tail = tails[:, head : head + 1]
         grad_key_ref[:, cols] = (
-            key_part_ref[:, cols] + tail * dot(value_ref[:, cols], low, 1, 1)
+            key_part_ref[:, cols] + tail * dot(value_ref[:, cols], low[cols], 1, 1)
         ).astype(BF16)
         grad_value_ref[:, cols] = (
-            value_part_ref[:, cols] + tail * dot(key_ref[:, cols], low, 1, 0)
+            value_part_ref[:, cols] + tail * dot(key_ref[:, cols], low[cols], 1, 0)
         ).astype(BF16)
+        for which, (source, target) in enumerate(
+            ((grad_key_ref, grad_key_out), (grad_value_ref, grad_value_out))
+        ):
+            store = pltpu.make_async_copy(
+                source.at[:, cols], target.at[:, cols], semaphores.at[2 * head + which]
+            )
+            store.start()
+            stores.append(store)
+    for store in stores:
+        store.wait()
 
 
 def on_device(blocks, groups, queries, key_rows, values, log_decay, norm_gain, grad_normed):
@@ -257,25 +373,47 @@
     def swap(array, axis):
         return lax.all_to_all(array, axis, 0, 0, tiled=True)
 
-    first, row, column = call(
+    whole = (length, width)
+    block = pltpu.VMEM(whole, BF16)
+    three = [block, block, block, pltpu.SemaphoreType.DMA((3, heads))]
+    first, row = call(
         update_kernel,
-        [like((blocks, rows + 8, HD)), like((8, length)), like((length, HD))],
+        [like((blocks, rows + 8, HD)), like((8, length))],
         log_decay,
         key_rows,
         values,
         flops=narrow,
+        places_in={0: pltpu.HBM, 1: pltpu.HBM, 2: pltpu.HBM},
+        scratch=[
+            pltpu.VMEM(log_decay.shape, F32),
+            pltpu.SemaphoreType.DMA,
+            block,
+            block,
+            pltpu.SemaphoreType.DMA((2, heads)),
+        ],
     )
     got = swap(first, "ctx")
-    (local,) = call(
-        local_kernel, [like((length, width))], queries, key_rows, values, row, column, flops=2 * square
+    local, column, gain = call(
+        local_kernel,
+        [like(whole), like((length, HD)), like((8, width))],
+        queries,
+        key_rows,
+        values,
+        row,
+        gain,
+        flops=2 * square,
+        places_in={0: pltpu.HBM, 1: pltpu.HBM, 2: pltpu.HBM},
+        scratch=three,
     )
     states, totals = call(
-        forward_kernel, [like((blocks, rows, HD)), like((blocks, 8, HD))], got
-    )
-    state_in = swap(states, "ctx").reshape(heads * HD, HD)
-    output, sums = call(
+        forward_kernel,
+        [like((blocks, rows, HD)), like((blocks, 8, HD))],
+        got,
+    )
+    state_in = swap(states, "ctx")
+    output, sums, low = call(
         output_kernel,
-        [like((length, width)), like((groups, 2 * length // HD, HD))],
+        [like(whole), like((groups, 2 * length // HD, HD)), like((heads * HD, HD), BF16)],
         queries,
         local,
         state_in,
@@ -287,7 +425,7 @@
     sums = swap(sums, "head")
     grad, second = call(
         grad_kernel,
-        [like((length, width), BF16), like((blocks, rows, HD))],
+        [like(whole, BF16), like((blocks, rows, HD))],
         sums,
         output,
         grad_normed,
@@ -297,30 +435,39 @@
         flops=narrow,
     )
     got = swap(second, "ctx")
+    (states,) = call(
+        backward_kernel,
+        [like((blocks, rows, HD))],
+        got,
+        totals,
+    )
+    state_out = swap(states, "ctx")
     grad_query, key_part, value_part = call(
         pull_kernel,
-        [like((length, width), BF16), like((length, width)), like((length, width))],
+        [like(whole, BF16), like(whole), like(whole)],
         queries,
         key_rows,
         values,
         grad,
-        state_in,
+        low,
         row,
-        column,
         flops=5 * square,
-    )
-    (states,) = call(backward_kernel, [like((blocks, rows, HD))], got, totals)
-    state_out = swap(states, "ctx").reshape(heads * HD, HD)
+        places_in={0: pltpu.HBM, 1: pltpu.HBM, 2: pltpu.HBM},
+        places_out={0: pltpu.HBM},
+        scratch=[*three, block, pltpu.SemaphoreType.DMA((heads,))],
+    )
     grad_key, grad_value = call(
         finish_kernel,
-        [like((length, width), BF16), like((length, width), BF16)],
+        [like(whole, BF16), like(whole, BF16)],
         key_part,
         value_part,
         key_rows,
         values,
         state_out,
-        column,
+        row,
         flops=2 * narrow,
+        places_out={0: pltpu.HBM, 1: pltpu.HBM},
+        scratch=[block, block, pltpu.SemaphoreType.DMA((2 * heads,))],
     )
     return grad_query, grad_key, grad_value
 

time: 106 us -> 93 us (0.88)
  Pallas kernels: 27.4 us -> 16.7 us
  blocking collectives: 60.9 us -> 59.2 us
    pallas_call x8, Pallas kernels: 27.4 us -> 16.7 us  [call(): pl.pallas_call(body, out_shape=[places_out[i](s.shape, s.dtype) if i in p...]
    all_to_all x3, blocking collectives: 60.9 us -> 59.2 us  [swap(): return lax.all_to_all(array, axis, 0, 0, tiled=True)]
where the time goes in v2:
time: 93 us; the launch traced here: 92.5 us
  blocking collectives  59.2 us (64%)
  Pallas kernels  16.7 us (18%)
  starting transfers between devices  7.37 us (8%)
  waiting for transfers between devices  6.86 us (7%)
  local copies, waits for them, and re-layouts  1.73 us (2%)
    all_to_all x3, blocking collectives, swap(): return lax.all_to_all(array, axis, 0, 0, tiled=True)  59.2 us
    pallas_call x8, Pallas kernels, call(): pl.pallas_call(body, out_shape=[places_out[i](s.shape, s.dtype) if i in p...  16.7 us
    all_to_all x2, starting transfers between devices, swap(): return lax.all_to_all(array, axis, 0, 0, tiled=True)  7.37 us
    all_to_all x2, waiting for transfers between devices, swap(): return lax.all_to_all(array, axis, 0, 0, tiled=True)  6.86 us
  transfers between devices with their start and end apart: 2, of which 2 were waited for; matrix products, arithmetic and copies ran while one was open for 0% of the time, Pallas kernels for 10%

profile of v2, /device:TPU:1, one launch (start us, length us, event | category | flops | bytes accessed | tf_op | source)
XLA Modules:
  0.0 92.5 jit_solution(9681647791328156042)
XLA Ops:
  0.6 2.6 %shard_map.85 = (f32[32,24,128]{2,1,0:T(8,128)S(1)}, f32[8,512]{1,0:T(8,128)S(1)}) custom-call(f32[4,512]{1,0:T(4,128)} %log_in.1, bf16[512,512]{1,0:T(8,128)(2,1)} %key_ref.1, bf16[512,512]{1,0:T(8,128)(2,1)} %value_ref.1), custom_call_target="tpu_custom_call" | custom-call | flops 67108864 | bytes 1466368 | tf_op jit(solution)/shard_map/pallas_call | solution.py:34
  3.2 19.9 %all_to_all.25.got_ref = f32[32,24,128]{2,1,0:T(8,128)S(1)} all-to-all(f32[32,24,128]{2,1,0:T(8,128)S(1)} %get-tuple-element.22), channel_id=1, replica_groups=mesh['ctx'=32,'head'=16] {'ctx'}, dimensions={0} | all-to-all | bytes 786432 | tf_op jit(solution)/shard_map/all_to_all | solution.py:374
  23.1 0.8 shard_map.87
  23.9 3.7 %all-to-all-start.1 = ((f32[32,16,128]{2,1,0:T(8,128)}), f32[32,16,128]{2,1,0:T(8,128)S(1)}, u32[]{:S(2)}, u32[]{:S(2)}) async-start(f32[32,16,128]{2,1,0:T(8,128)} %get-tuple-element.23), calls=%async_computation.1 | async-start | bytes 524288 | tf_op jit(solution)/shard_map/all_to_all | solution.py:374
  27.6 0.0 copy-start.6
  27.6 0.7 copy-done.6
  28.3 0.0 copy-start
  28.3 0.0 copy-start.1
  28.3 3.4 %shard_map.86 = (f32[512,512]{1,0:T(8,128)S(1)}, f32[512,128]{1,0:T(8,128)S(1)}, f32[8,512]{1,0:T(8,128)S(1)}) custom-call(bf16[512,512]{1,0:T(8,128)(2,1)} %query_in.3, bf16[512,512]{1,0:T(8,128)(2,1)} %key_ref.1, bf16[512,512]{1,0:T(8,128)(2,1)} %value_ref.1, f32[8,512]{1,0:T(8,128)S(1)} %get-tuple-element.20.row_ref, f32[1,512]{1,0:T(1,128)S(1)} %bitcast.1), custom_call_target="tpu_custom_call" | custom-call | flops 536870912 | bytes 2918400 | tf_op jit(solution)/shard_map/pallas_call | solution.py:34
  31.7 4.8 %all-to-all-done.1.state_ref = f32[32,16,128]{2,1,0:T(8,128)S(1)} async-done(((f32[32,16,128]{2,1,0:T(8,128)}), f32[32,16,128]{2,1,0:T(8,128)S(1)}, u32[]{:S(2)}, u32[]{:S(2)}) %all-to-all-start.1) | async-done | bytes 262176 | tf_op jit(solution)/shard_map/all_to_all | solution.py:374
  36.4 0.0 copy-done
  36.4 0.0 copy-done.1
  36.4 0.6 shard_map.88
  37.0 25.1 %all_to_all.26.sums_ref = f32[16,8,128]{2,1,0:T(8,128)S(1)} all-to-all(f32[16,8,128]{2,1,0:T(8,128)S(1)} %get-tuple-element.26), channel_id=1, replica_groups=mesh['ctx'=32,'head'=16] {'head'}, dimensions={0} | all-to-all | bytes 131072 | tf_op jit(solution)/shard_map/all_to_all | solution.py:374
  62.1 1.1 %shard_map.89 = (bf16[512,512]{1,0:T(8,128)(2,1)S(1)}, f32[32,16,128]{2,1,0:T(8,128)S(1)}) custom-call(f32[16,8,128]{2,1,0:T(8,128)S(1)} %all_to_all.26.sums_ref, f32[512,512]{1,0:T(8,128)S(1)} %get-tuple-element.27.output_ref, bf16[512,512]{1,0:T(8,128)(2,1)S(1)} %copy-done, f32[8,512]{1,0:T(8,128)S(1)} %get-tuple-element.25.gain_ref, ...), custom_call_target="tpu_custom_call" | custom-call | flops 67108864 | bytes 3227648 | tf_op jit(solution)/shard_map/pallas_call | solution.py:34
  63.3 0.0 copy-start.4
  63.3 14.1 %all_to_all.27.got_ref = f32[32,16,128]{2,1,0:T(8,128)S(1)} all-to-all(f32[32,16,128]{2,1,0:T(8,128)S(1)} %get-tuple-element.33), channel_id=1, replica_groups=mesh['ctx'=32,'head'=16] {'ctx'}, dimensions={0} | all-to-all | bytes 524288 | tf_op jit(solution)/shard_map/all_to_all | solution.py:374
  77.5 0.0 copy-done.4
  77.5 0.8 shard_map.91
  78.2 3.7 %all-to-all-start.4 = ((f32[32,16,128]{2,1,0:T(8,128)}), f32[32,16,128]{2,1,0:T(8,128)S(1)}, u32[]{:S(2)}, u32[]{:S(2)}) async-start(f32[32,16,128]{2,1,0:T(8,128)} %shard_map.91), calls=%async_computation.4 | async-start | bytes 524288 | tf_op jit(solution)/shard_map/all_to_all | solution.py:374
  82.0 0.0 copy-start.5
  82.0 1.0 %copy-done.5 = bf16[512,512]{1,0:T(8,128)(2,1)S(1)} copy-done((bf16[512,512]{1,0:T(8,128)(2,1)S(1)}, bf16[512,512]{1,0:T(8,128)(2,1)}, u32[]{:S(2)}) %copy-start.5) | copy-done | bytes 524312
  83.0 0.0 copy-start.2
  83.0 0.0 copy-start.3
  83.0 5.9 %shard_map.90 = (bf16[512,512]{1,0:T(8,128)(2,1)}, f32[512,512]{1,0:T(8,128)S(1)}, f32[512,512]{1,0:T(8,128)S(1)}) custom-call(bf16[512,512]{1,0:T(8,128)(2,1)} %query_in.3, bf16[512,512]{1,0:T(8,128)(2,1)} %key_ref.1, bf16[512,512]{1,0:T(8,128)(2,1)} %value_ref.1, bf16[512,512]{1,0:T(8,128)(2,1)S(1)} %copy-done.5, ...), custom_call_target="tpu_custom_call" | custom-call | flops 1342177280 | bytes 4866048 | tf_op jit(solution)/shard_map/pallas_call | solution.py:34
  89.0 2.1 %all-to-all-done.4.state_ref = f32[32,16,128]{2,1,0:T(8,128)S(1)} async-done(((f32[32,16,128]{2,1,0:T(8,128)}), f32[32,16,128]{2,1,0:T(8,128)S(1)}, u32[]{:S(2)}, u32[]{:S(2)}) %all-to-all-start.4) | async-done | bytes 262176 | tf_op jit(solution)/shard_map/all_to_all | solution.py:374
  91.1 0.0 copy-done.2
  91.1 0.0 copy-done.3
  91.1 1.4 %shard_map.92 = (bf16[512,512]{1,0:T(8,128)(2,1)}, bf16[512,512]{1,0:T(8,128)(2,1)}) custom-call(f32[512,512]{1,0:T(8,128)S(1)} %get-tuple-element.31.key_part_ref, f32[512,512]{1,0:T(8,128)S(1)} %get-tuple-element.32.value_part_ref, bf16[512,512]{1,0:T(8,128)(2,1)S(1)} %copy-done.2, bf16[512,512]{1,0:T(8,128)(2,1)S(1)} %copy-done.3, ...), custom_call_target="tpu_custom_call" | custom-call | flops 134217728 | bytes 4472832 | tf_op jit(solution)/shard_map/pallas_call | solution.py:34
Async XLA Ops:
  23.9 12.5 %all-to-all-start.1 = ((f32[32,16,128]{2,1,0:T(8,128)}), f32[32,16,128]{2,1,0:T(8,128)S(1)}, u32[]{:S(2)}, u32[]{:S(2)}) async-start(f32[32,16,128]{2,1,0:T(8,128)} %get-tuple-element.23), calls=%async_computation.1 | async-start | bytes 524288 | tf_op jit(solution)/shard_map/all_to_all | solution.py:374
  27.6 0.7 copy-start.6
  28.3 8.2 %copy-start = (bf16[512,512]{1,0:T(8,128)(2,1)S(1)}, bf16[512,512]{1,0:T(8,128)(2,1)}, u32[]{:S(2)}) copy-start(bf16[512,512]{1,0:T(8,128)(2,1)} %normed_ref.3) | copy-start | bytes 1572868
  28.3 8.2 %copy-start.1 = (bf16[512,512]{1,0:T(8,128)(2,1)S(1)}, bf16[512,512]{1,0:T(8,128)(2,1)}, u32[]{:S(2)}) copy-start(bf16[512,512]{1,0:T(8,128)(2,1)} %query_in.3) | copy-start | bytes 1572868
  63.3 14.2 %copy-start.4 = (bf16[512,512]{1,0:T(8,128)(2,1)}, bf16[512,512]{1,0:T(8,128)(2,1)S(1)}, u32[]{:S(2)}) copy-start(bf16[512,512]{1,0:T(8,128)(2,1)S(1)} %get-tuple-element.28.grad_ref) | copy-start | bytes 1572868
  78.2 12.8 %all-to-all-start.4 = ((f32[32,16,128]{2,1,0:T(8,128)}), f32[32,16,128]{2,1,0:T(8,128)S(1)}, u32[]{:S(2)}, u32[]{:S(2)}) async-start(f32[32,16,128]{2,1,0:T(8,128)} %shard_map.91), calls=%async_computation.4 | async-start | bytes 524288 | tf_op jit(solution)/shard_map/all_to_all | solution.py:374
  82.0 1.0 %copy-start.5 = (bf16[512,512]{1,0:T(8,128)(2,1)S(1)}, bf16[512,512]{1,0:T(8,128)(2,1)}, u32[]{:S(2)}) copy-start(bf16[512,512]{1,0:T(8,128)(2,1)} %copy-done.4) | copy-start | bytes 1572868
  83.0 8.1 %copy-start.2 = (bf16[512,512]{1,0:T(8,128)(2,1)S(1)}, bf16[512,512]{1,0:T(8,128)(2,1)}, u32[]{:S(2)}) copy-start(bf16[512,512]{1,0:T(8,128)(2,1)} %key_ref.1) | copy-start | bytes 1572868
  83.0 8.1 %copy-start.3 = (bf16[512,512]{1,0:T(8,128)(2,1)S(1)}, bf16[512,512]{1,0:T(8,128)(2,1)}, u32[]{:S(2)}) copy-start(bf16[512,512]{1,0:T(8,128)(2,1)} %value_ref.1) | copy-start | bytes 1572868

commit v3 on v2

--- a/solution.py
+++ b/solution.py
@@ -1,3 +1,5 @@
+import functools
+
 import jax
 import jax.numpy as jnp
 from jax import lax
@@ -62,23 +64,18 @@
     return jnp.exp(running[:, running.shape[1] - 1 :] - running)
 
 
-def load_columns(sources, buffers, semaphores):
-    copies = []
-    for which, (source, buffer) in enumerate(zip(sources, buffers)):
-        copies.append([])
-        for head in range(source.shape[1] // HD):
-            cols = head_columns(head)
-            copy = pltpu.make_async_copy(
-                source.at[:, cols], buffer.at[:, cols], semaphores.at[which, head]
-            )
-            copies[which].append(copy)
-    for head in zip(*copies):
-        for copy in head:
-            copy.start()
-    return copies
+def load_all(sources, buffers, semaphores):
+    loads = [
+        pltpu.make_async_copy(source, buffer, semaphores.at[i])
+        for i, (source, buffer) in enumerate(zip(sources, buffers))
+    ]
+    for load in loads:
+        load.start()
+    return loads
 
 
 def update_kernel(
+    targets,
     log_in,
     key_in,
     value_in,
@@ -92,7 +89,7 @@
 ):
     load_logs = pltpu.make_async_copy(log_in, log_ref, log_semaphore)
     load_logs.start()
-    loads = load_columns((key_in, value_in), (key_ref, value_ref), semaphores)
+    loads = load_all((key_in, value_in), (key_ref, value_ref), semaphores)
     heads, length = log_ref.shape
     load_logs.wait()
     logs = jnp.concatenate([log_ref[...], jnp.zeros((8 - heads, length), F32)], axis=0)
@@ -117,32 +114,32 @@
     running = jnp.concatenate(parts, axis=1)
     row_ref[...] = running
     tail = jnp.exp(offset - running)
-    targets, rows = send_ref.shape[0], send_ref.shape[1] - 8
     per_head = targets // heads
+    rows = heads * HD // targets
+    for target in range(targets):
+        last = target * (rows + 1) + rows
+        head = target // per_head
+        send_ref[last : last + 1] = jnp.broadcast_to(offset[head : head + 1], (1, HD))
+    for load in loads:
+        load.wait()
     for head in range(heads):
-        here = slice(head * per_head, (head + 1) * per_head)
-        send_ref[here, rows:] = jnp.broadcast_to(
-            offset[head : head + 1][None], (per_head, 8, HD)
-        )
-    for head in range(heads):
-        for load in loads:
-            load[head].wait()
         turned = key_ref[:, head_columns(head)].T.astype(F32)
         scaled = (turned * tail[head : head + 1]).astype(BF16)
         update = dot(scaled, value_ref[:, head_columns(head)], 1, 0)
-        here = slice(head * per_head, (head + 1) * per_head)
-        send_ref[here, :rows] = update.reshape(per_head, rows, HD)
+        for i in range(per_head):
+            first = (head * per_head + i) * (rows + 1)
+            send_ref[first : first + rows] = update[i * rows : (i + 1) * rows]
 
 
 def forward_kernel(got_ref, send_ref, total_ref):
     blocks, rows = send_ref.shape[:2]
-    totals = got_ref[:, rows : rows + 1, :]
-    total_ref[...] = jnp.broadcast_to(totals, total_ref.shape)
-    factors = jnp.exp(totals)
     state = jnp.zeros((rows, HD), F32)
     for block in range(blocks):
+        first = block * (rows + 1)
         send_ref[block] = state
-        state = factors[block] * state + got_ref[block, :rows]
+        total = got_ref[first + rows : first + rows + 1]
+        total_ref[block] = jnp.broadcast_to(total, total_ref.shape[1:])
+        state = jnp.exp(total) * state + got_ref[first : first + rows]
 
 
 def backward_kernel(got_ref, total_ref, send_ref):
@@ -184,23 +181,30 @@
     local_ref,
     column_ref,
     gain_ref,
+    turned_out,
     query_ref,
     key_ref,
     value_ref,
     semaphores,
+    turned_ref,
+    store_semaphore,
 ):
     length = query_ref.shape[0]
-    loads = load_columns(
-        (query_in, key_in, value_in), (query_ref, key_ref, value_ref), semaphores
-    )
+    loads = load_all((query_in, key_in, value_in), (query_ref, key_ref, value_ref), semaphores)
     gain_ref[...] = jnp.broadcast_to(gain_in[...], gain_ref.shape)
     running = row_ref[...]
     column_ref[...] = jnp.concatenate(
         [running, jnp.exp(running), jnp.zeros((HD - 16, length), F32)], axis=0
     ).T
+    for load in loads:
+        load.wait()
     for head in range(query_ref.shape[1] // HD):
-        for load in loads:
-            load[head].wait()
+        cols = head_columns(head)
+        grown = jnp.exp(running[head : head + 1])
+        turned_ref[cols] = (query_ref[:, cols].T.astype(F32) * grown).astype(BF16)
+    store = pltpu.make_async_copy(turned_ref, turned_out, store_semaphore)
+    store.start()
+    for head in range(query_ref.shape[1] // HD):
         cols = head_columns(head)
         sums = {}
         for t, j, diagonal in tiles(length):
@@ -213,6 +217,7 @@
             sums[t.start] = sums[t.start] + part if t.start in sums else part
         for start, value in sums.items():
             local_ref[start : start + TILE, cols] = value
+    store.wait()
 
 
 def output_kernel(
@@ -238,20 +243,22 @@
     send_ref[...] = jnp.broadcast_to(packed[None], send_ref.shape)
 
 
-def grad_kernel(
-    sums_ref, output_ref, normed_ref, gain_ref, query_ref, column_ref, grad_ref, send_ref
-):
-    length = query_ref.shape[0]
-    heads = query_ref.shape[1] // HD
+def grad_kernel(sums_ref, output_ref, normed_ref, gain_ref, turned_ref, grad_ref, send_ref):
+    length, width = output_ref.shape
+    heads = width // HD
     pieces = length // HD
-    channels = sums_ref.shape[0] * heads * HD
+    channels = sums_ref.shape[0] * width
     sums = jnp.sum(sums_ref[...], axis=0)
     inverse = lax.rsqrt(sums[:pieces] / channels + EPSILON)
     inner = sums[pieces:] / channels
     scale = inverse * inverse * inverse * inner
-    both = jnp.concatenate([inverse, scale, jnp.zeros((HD - 2 * pieces, HD), F32)], axis=0).T
-    inverse = jnp.concatenate([both[:, i : i + 1] for i in range(pieces)], axis=0)
-    scale = jnp.concatenate([both[:, pieces + i : pieces + i + 1] for i in range(pieces)], axis=0)
+
+    def down(rows):
+        return jnp.concatenate(
+            [jnp.broadcast_to(rows[i : i + 1], (HD, HD)).T for i in range(pieces)], axis=0
+        )
+
+    inverse, scale = down(inverse), down(scale)
     targets, rows = send_ref.shape[:2]
     per_head = targets // heads
     for head in range(heads):
@@ -259,10 +266,9 @@
         gained = normed_ref[:, cols].astype(F32) * gain_ref[:1, cols]
         grad = (inverse * gained - output_ref[:, cols] * scale).astype(BF16)
         grad_ref[:, cols] = grad
-        scaled = (query_ref[:, cols].astype(F32) * column_ref[:, 8 + head : 9 + head]).astype(BF16)
-        send_ref[head * per_head : (head + 1) * per_head] = dot(scaled, grad, 0, 0).reshape(
-            per_head, rows, HD
-        )
+        send_ref[head * per_head : (head + 1) * per_head] = dot(
+            turned_ref[cols], grad, 1, 0
+        ).reshape(per_head, rows, HD)
 
 
 def add(sums, where, part):
@@ -287,14 +293,12 @@
     store_semaphores,
 ):
     length = query_ref.shape[0]
-    loads = load_columns(
-        (query_in, key_in, value_in), (query_ref, key_ref, value_ref), semaphores
-    )
+    loads = load_all((query_in, key_in, value_in), (query_ref, key_ref, value_ref), semaphores)
     stores = []
     columns, grown = turn(row_ref[...]), turn(jnp.exp(row_ref[...]))
+    for load in loads:
+        load.wait()
     for head in range(query_ref.shape[1] // HD):
-        for load in loads:
-            load[head].wait()
         cols = head_columns(head)
         query_sums, key_sums, value_sums = {}, {}, {}
         for t, j, diagonal in tiles(length):
@@ -375,10 +379,10 @@
 
     whole = (length, width)
     block = pltpu.VMEM(whole, BF16)
-    three = [block, block, block, pltpu.SemaphoreType.DMA((3, heads))]
+    three = [block, block, block, pltpu.SemaphoreType.DMA((3,))]
     first, row = call(
-        update_kernel,
-        [like((blocks, rows + 8, HD)), like((8, length))],
+        functools.partial(update_kernel, blocks),
+        [like((blocks * (rows + 1), HD)), like((8, length))],
         log_decay,
         key_rows,
         values,
@@ -389,13 +393,13 @@
             pltpu.SemaphoreType.DMA,
             block,
             block,
-            pltpu.SemaphoreType.DMA((2, heads)),
+            pltpu.SemaphoreType.DMA((2,)),
         ],
     )
-    got = swap(first, "ctx")
-    local, column, gain = call(
+    got = swap(first.reshape(blocks, rows + 1, 1, HD), "ctx").reshape(first.shape)
+    local, column, gain, turned = call(
         local_kernel,
-        [like(whole), like((length, HD)), like((8, width))],
+        [like(whole), like((length, HD)), like((8, width)), like((width, length), BF16)],
         queries,
         key_rows,
         values,
@@ -403,7 +407,8 @@
         gain,
         flops=2 * square,
         places_in={0: pltpu.HBM, 1: pltpu.HBM, 2: pltpu.HBM},
-        scratch=three,
+        places_out={3: pltpu.HBM},
+        scratch=[*three, pltpu.VMEM((width, length), BF16), pltpu.SemaphoreType.DMA],
     )
     states, totals = call(
         forward_kernel,
@@ -430,8 +435,7 @@
         output,
         grad_normed,
         gain,
-        queries,
-        column,
+        turned,
         flops=narrow,
     )
     got = swap(second, "ctx")

time: 93 us -> 90.6 us (0.974)
  blocking collectives: 59.2 us -> 57.9 us
  Pallas kernels: 16.7 us -> 15.4 us
    pallas_call x8, Pallas kernels: 16.7 us -> 15.4 us  [call(): pl.pallas_call(body, out_shape=[places_out[i](s.shape, s.dtype) if i in p...]
    all_to_all x3, blocking collectives: 59.2 us -> 57.9 us  [swap(): return lax.all_to_all(array, axis, 0, 0, tiled=True)]
  transfers between devices with their start and end apart: 2 -> 2, of which waited for: 2 -> 2; matrix products, arithmetic and copies ran while one was open for 0% -> 0% of each run, Pallas kernels for 10% -> 11%
where the time goes in v3:
time: 90.6 us; the launch traced here: 90.1 us
  blocking collectives  57.9 us (64%)
  Pallas kernels  15.4 us (17%)
  starting transfers between devices  7.39 us (8%)
  waiting for transfers between devices  6.96 us (8%)
  local copies, waits for them, and re-layouts  1.74 us (2%)
    all_to_all x3, blocking collectives, swap(): return lax.all_to_all(array, axis, 0, 0, tiled=True)  57.9 us
    pallas_call x8, Pallas kernels, call(): pl.pallas_call(body, out_shape=[places_out[i](s.shape, s.dtype) if i in p...  15.4 us
    all_to_all x2, starting transfers between devices, swap(): return lax.all_to_all(array, axis, 0, 0, tiled=True)  7.39 us
    all_to_all x2, waiting for transfers between devices, swap(): return lax.all_to_all(array, axis, 0, 0, tiled=True)  6.96 us
  transfers between devices with their start and end apart: 2, of which 2 were waited for; matrix products, arithmetic and copies ran while one was open for 0% of the time, Pallas kernels for 11%

profile of v3, /device:TPU:1, one launch (start us, length us, event | category | flops | bytes accessed | tf_op | source)
XLA Modules:
  0.0 90.1 jit_solution(17692124854023597319)
XLA Ops:
  0.6 1.7 %shard_map.85 = (f32[544,128]{1,0:T(8,128)S(1)}, f32[8,512]{1,0:T(8,128)S(1)}) custom-call(f32[4,512]{1,0:T(4,128)} %log_in.1, bf16[512,512]{1,0:T(8,128)(2,1)} %key_ref.1, bf16[512,512]{1,0:T(8,128)(2,1)} %value_ref.1), custom_call_target="tpu_custom_call" | custom-call | flops 67108864 | bytes 1351680 | tf_op jit(solution)/shard_map/pallas_call | solution.py:36
  2.3 18.8 %all_to_all.25 = f32[32,17,1,128]{3,2,1,0:T(1,128)S(1)} all-to-all(f32[32,17,1,128]{3,2,1,0:T(1,128)S(1)} %bitcast.4), channel_id=1, replica_groups=mesh['ctx'=32,'head'=16] {'ctx'}, dimensions={0} | all-to-all | bytes 557056 | tf_op jit(solution)/shard_map/all_to_all | solution.py:378
  21.1 0.8 shard_map.87
  21.9 3.7 %all-to-all-start.1 = ((f32[32,16,128]{2,1,0:T(8,128)}), f32[32,16,128]{2,1,0:T(8,128)S(1)}, u32[]{:S(2)}, u32[]{:S(2)}) async-start(f32[32,16,128]{2,1,0:T(8,128)} %get-tuple-element.24), calls=%async_computation.1 | async-start | bytes 524288 | tf_op jit(solution)/shard_map/all_to_all | solution.py:378
  25.6 0.0 copy-start.7
  25.6 0.7 copy-done.7
  26.3 0.0 copy-start
  26.3 0.0 copy-start.3
  26.3 3.8 %shard_map.86 = (f32[512,512]{1,0:T(8,128)S(1)}, f32[512,128]{1,0:T(8,128)S(1)}, f32[8,512]{1,0:T(8,128)S(1)}, bf16[512,512]{1,0:T(8,128)(2,1)}) custom-call(bf16[512,512]{1,0:T(8,128)(2,1)} %query_in.3, bf16[512,512]{1,0:T(8,128)(2,1)} %key_ref.1, bf16[512,512]{1,0:T(8,128)(2,1)} %value_ref.1, f32[8,512]{1,0:T(8,128)S(1)} %get-tuple-element.21.row_ref, ...), custom_call_target="tpu_custom_call" | custom-call | flops 536870912 | bytes 3442688 | tf_op jit(solution)/shard_map/pallas_call | solution.py:36
  30.1 4.6 %all-to-all-done.1.state_ref = f32[32,16,128]{2,1,0:T(8,128)S(1)} async-done(((f32[32,16,128]{2,1,0:T(8,128)}), f32[32,16,128]{2,1,0:T(8,128)S(1)}, u32[]{:S(2)}, u32[]{:S(2)}) %all-to-all-start.1) | async-done | bytes 262176 | tf_op jit(solution)/shard_map/all_to_all | solution.py:378
  34.7 0.0 copy-done
  34.7 0.0 copy-done.3
  34.7 0.0 copy-start.4
  34.7 0.6 shard_map.88
  35.3 25.1 %all_to_all.26.sums_ref = f32[16,8,128]{2,1,0:T(8,128)S(1)} all-to-all(f32[16,8,128]{2,1,0:T(8,128)S(1)} %get-tuple-element.27), channel_id=1, replica_groups=mesh['ctx'=32,'head'=16] {'head'}, dimensions={0} | all-to-all | bytes 131072 | tf_op jit(solution)/shard_map/all_to_all | solution.py:378
  60.4 0.0 copy-done.4
  60.4 0.6 shard_map.89
  61.0 0.0 copy-start.5
  61.0 14.1 %all_to_all.27.got_ref = f32[32,16,128]{2,1,0:T(8,128)S(1)} all-to-all(f32[32,16,128]{2,1,0:T(8,128)S(1)} %get-tuple-element.35), channel_id=1, replica_groups=mesh['ctx'=32,'head'=16] {'ctx'}, dimensions={0} | all-to-all | bytes 524288 | tf_op jit(solution)/shard_map/all_to_all | solution.py:378
  75.1 0.8 shard_map.91
  75.8 0.0 copy-done.5
  75.8 3.7 %all-to-all-start.4 = ((f32[32,16,128]{2,1,0:T(8,128)}), f32[32,16,128]{2,1,0:T(8,128)S(1)}, u32[]{:S(2)}, u32[]{:S(2)}) async-start(f32[32,16,128]{2,1,0:T(8,128)} %shard_map.91), calls=%async_computation.4 | async-start | bytes 524288 | tf_op jit(solution)/shard_map/all_to_all | solution.py:378
  79.6 0.0 copy-start.6
  79.6 1.0 %copy-done.6 = bf16[512,512]{1,0:T(8,128)(2,1)S(1)} copy-done((bf16[512,512]{1,0:T(8,128)(2,1)S(1)}, bf16[512,512]{1,0:T(8,128)(2,1)}, u32[]{:S(2)}) %copy-start.6) | copy-done | bytes 524312
  80.6 0.0 copy-start.1
  80.6 0.0 copy-start.2
  80.6 5.6 %shard_map.90 = (bf16[512,512]{1,0:T(8,128)(2,1)}, f32[512,512]{1,0:T(8,128)S(1)}, f32[512,512]{1,0:T(8,128)S(1)}) custom-call(bf16[512,512]{1,0:T(8,128)(2,1)} %query_in.3, bf16[512,512]{1,0:T(8,128)(2,1)} %key_ref.1, bf16[512,512]{1,0:T(8,128)(2,1)} %value_ref.1, bf16[512,512]{1,0:T(8,128)(2,1)S(1)} %copy-done.6, ...), custom_call_target="tpu_custom_call" | custom-call | flops 1342177280 | bytes 4866048 | tf_op jit(solution)/shard_map/pallas_call | solution.py:36
  86.3 2.4 %all-to-all-done.4.state_ref = f32[32,16,128]{2,1,0:T(8,128)S(1)} async-done(((f32[32,16,128]{2,1,0:T(8,128)}), f32[32,16,128]{2,1,0:T(8,128)S(1)}, u32[]{:S(2)}, u32[]{:S(2)}) %all-to-all-start.4) | async-done | bytes 262176 | tf_op jit(solution)/shard_map/all_to_all | solution.py:378
  88.7 0.0 copy-done.1
  88.7 0.0 copy-done.2
  88.7 1.4 %shard_map.92 = (bf16[512,512]{1,0:T(8,128)(2,1)}, bf16[512,512]{1,0:T(8,128)(2,1)}) custom-call(f32[512,512]{1,0:T(8,128)S(1)} %get-tuple-element.33.key_part_ref, f32[512,512]{1,0:T(8,128)S(1)} %get-tuple-element.34.value_part_ref, bf16[512,512]{1,0:T(8,128)(2,1)S(1)} %copy-done.1, bf16[512,512]{1,0:T(8,128)(2,1)S(1)} %copy-done.2, ...), custom_call_target="tpu_custom_call" | custom-call | flops 134217728 | bytes 4472832 | tf_op jit(solution)/shard_map/pallas_call | solution.py:36
Async XLA Ops:
  21.9 12.8 %all-to-all-start.1 = ((f32[32,16,128]{2,1,0:T(8,128)}), f32[32,16,128]{2,1,0:T(8,128)S(1)}, u32[]{:S(2)}, u32[]{:S(2)}) async-start(f32[32,16,128]{2,1,0:T(8,128)} %get-tuple-element.24), calls=%async_computation.1 | async-start | bytes 524288 | tf_op jit(solution)/shard_map/all_to_all | solution.py:378
  25.6 0.7 copy-start.7
  26.3 8.4 %copy-start = (bf16[512,512]{1,0:T(8,128)(2,1)S(1)}, bf16[512,512]{1,0:T(8,128)(2,1)}, u32[]{:S(2)}) copy-start(bf16[512,512]{1,0:T(8,128)(2,1)} %normed_ref.3) | copy-start | bytes 1572868
  26.3 8.4 %copy-start.3 = (bf16[512,512]{1,0:T(8,128)(2,1)S(1)}, bf16[512,512]{1,0:T(8,128)(2,1)}, u32[]{:S(2)}) copy-start(bf16[512,512]{1,0:T(8,128)(2,1)} %query_in.3) | copy-start | bytes 1572868
  34.7 25.7 %copy-start.4 = (bf16[512,512]{1,0:T(8,128)(2,1)S(1)}, bf16[512,512]{1,0:T(8,128)(2,1)}, u32[]{:S(2)}) copy-start(bf16[512,512]{1,0:T(8,128)(2,1)} %get-tuple-element.29.turned_ref) | copy-start | bytes 1572868
  61.0 14.9 %copy-start.5 = (bf16[512,512]{1,0:T(8,128)(2,1)}, bf16[512,512]{1,0:T(8,128)(2,1)S(1)}, u32[]{:S(2)}) copy-start(bf16[512,512]{1,0:T(8,128)(2,1)S(1)} %get-tuple-element.30.grad_ref) | copy-start | bytes 1572868
  75.8 12.8 %all-to-all-start.4 = ((f32[32,16,128]{2,1,0:T(8,128)}), f32[32,16,128]{2,1,0:T(8,128)S(1)}, u32[]{:S(2)}, u32[]{:S(2)}) async-start(f32[32,16,128]{2,1,0:T(8,128)} %shard_map.91), calls=%async_computation.4 | async-start | bytes 524288 | tf_op jit(solution)/shard_map/all_to_all | solution.py:378
  79.6 1.0 %copy-start.6 = (bf16[512,512]{1,0:T(8,128)(2,1)S(1)}, bf16[512,512]{1,0:T(8,128)(2,1)}, u32[]{:S(2)}) copy-start(bf16[512,512]{1,0:T(8,128)(2,1)} %copy-done.5) | copy-start | bytes 1572868
  80.6 8.1 %copy-start.1 = (bf16[512,512]{1,0:T(8,128)(2,1)S(1)}, bf16[512,512]{1,0:T(8,128)(2,1)}, u32[]{:S(2)}) copy-start(bf16[512,512]{1,0:T(8,128)(2,1)} %key_ref.1) | copy-start | bytes 1572868
  80.6 8.1 %copy-start.2 = (bf16[512,512]{1,0:T(8,128)(2,1)S(1)}, bf16[512,512]{1,0:T(8,128)(2,1)}, u32[]{:S(2)}) copy-start(bf16[512,512]{1,0:T(8,128)(2,1)} %value_ref.1) | copy-start | bytes 1572868

commit v4 on v3

--- a/solution.py
+++ b/solution.py
@@ -57,6 +57,22 @@
 
 def turn(rows):
     return jnp.concatenate([rows, jnp.zeros((HD - 8, rows.shape[1]), F32)], axis=0).T
+
+
+def down(pieces):
+    return jnp.concatenate(
+        [
+            jnp.broadcast_to(pieces[i : i + 1], (HD, HD)).T
+            for i in range(pieces.shape[0])
+        ],
+        axis=0,
+    )
+
+
+def cut(row):
+    return jnp.concatenate(
+        [row[:, head_columns(i)] for i in range(row.shape[1] // HD)], axis=0
+    )
 
 
 def tail_rows(row_ref):
@@ -179,7 +195,6 @@
     row_ref,
     gain_in,
     local_ref,
-    column_ref,
     gain_ref,
     turned_out,
     query_ref,
@@ -193,9 +208,7 @@
     loads = load_all((query_in, key_in, value_in), (query_ref, key_ref, value_ref), semaphores)
     gain_ref[...] = jnp.broadcast_to(gain_in[...], gain_ref.shape)
     running = row_ref[...]
-    column_ref[...] = jnp.concatenate(
-        [running, jnp.exp(running), jnp.zeros((HD - 16, length), F32)], axis=0
-    ).T
+    columns = turn(running)
     for load in loads:
         load.wait()
     for head in range(query_ref.shape[1] // HD):
@@ -209,7 +222,7 @@
         sums = {}
         for t, j, diagonal in tiles(length):
             within = within_block(
-                column_ref[t, head : head + 1], row_ref[head : head + 1, j], diagonal
+                columns[t, head : head + 1], row_ref[head : head + 1, j], diagonal
             )
             scores = dot(query_ref[t, cols], key_ref[j, cols], 1, 1)
             masked = (scores * within).astype(BF16)
@@ -221,16 +234,17 @@
 
 
 def output_kernel(
-    query_ref, local_ref, state_ref, column_ref, normed_ref, gain_ref, output_ref, send_ref, low_ref
+    query_ref, local_ref, state_ref, row_ref, normed_ref, gain_ref, output_ref, send_ref, low_ref
 ):
     length = query_ref.shape[0]
     low_ref[...] = state_ref[...].reshape(low_ref.shape).astype(BF16)
+    grown = jnp.exp(row_ref[...])
     squares = jnp.zeros((length, HD), F32)
     crosses = jnp.zeros((length, HD), F32)
     for head in range(query_ref.shape[1] // HD):
         cols = head_columns(head)
         carried = dot(query_ref[:, cols], low_ref[cols], 1, 0)
-        output = local_ref[:, cols] + column_ref[:, 8 + head : 9 + head] * carried
+        output = local_ref[:, cols] + down(cut(grown[head : head + 1])) * carried
         output_ref[:, cols] = output
         gained = normed_ref[:, cols].astype(F32) * gain_ref[:1, cols]
         squares = squares + output * output
@@ -252,11 +266,6 @@
     inverse = lax.rsqrt(sums[:pieces] / channels + EPSILON)
     inner = sums[pieces:] / channels
     scale = inverse * inverse * inverse * inner
-
-    def down(rows):
-        return jnp.concatenate(
-            [jnp.broadcast_to(rows[i : i + 1], (HD, HD)).T for i in range(pieces)], axis=0
-        )
 
     inverse, scale = down(inverse), down(scale)
     targets, rows = send_ref.shape[:2]
@@ -279,7 +288,7 @@
     query_in,
     key_in,
     value_in,
-    grad_ref,
+    grad_in,
     low_ref,
     row_ref,
     grad_query_out,
@@ -288,43 +297,44 @@
     query_ref,
     key_ref,
     value_ref,
+    grad_ref,
     semaphores,
     grad_query_ref,
     store_semaphores,
 ):
-    length = query_ref.shape[0]
-    loads = load_all((query_in, key_in, value_in), (query_ref, key_ref, value_ref), semaphores)
-    stores = []
+    length, width = query_ref.shape
+    loads = load_all((query_in, key_in, value_in, grad_in,), (query_ref, key_ref, value_ref, grad_ref,), semaphores)
     columns, grown = turn(row_ref[...]), turn(jnp.exp(row_ref[...]))
     for load in loads:
         load.wait()
-    for head in range(query_ref.shape[1] // HD):
+    stores = []
+    for head in range(width // HD):
         cols = head_columns(head)
         query_sums, key_sums, value_sums = {}, {}, {}
+        query_turned, grad_turned = query_ref[:, cols].T, grad_ref[:, cols].T
         for t, j, diagonal in tiles(length):
-            within = within_block(
-                columns[t, head : head + 1], row_ref[head : head + 1, j], diagonal
-            )
+            within = within_block(columns[t, head : head + 1], row_ref[head : head + 1, j], diagonal)
             query, key, grad = query_ref[t, cols], key_ref[j, cols], grad_ref[t, cols]
             pulled = (dot(grad, value_ref[j, cols], 1, 1) * within).astype(BF16)
             masked = (dot(query, key, 1, 1) * within).astype(BF16)
             add(query_sums, t.start, dot(pulled, key, 1, 0))
-            add(key_sums, j.start, dot(pulled, query, 0, 0))
-            add(value_sums, j.start, dot(masked, grad, 0, 0))
+            add(key_sums, j.start, dot(query_turned[:, t], pulled, 1, 0))
+            add(value_sums, j.start, dot(grad_turned[:, t], masked, 1, 0))
         for start in range(0, length, TILE):
             here = slice(start, start + TILE)
             carried = dot(grad_ref[here, cols], low_ref[cols], 1, 1)
             grad_query_ref[here, cols] = (
                 query_sums[start] + grown[here, head : head + 1] * carried
             ).astype(BF16)
-            key_part_ref[here, cols] = key_sums[start]
-            value_part_ref[here, cols] = value_sums[start]
         stores.append(
             pltpu.make_async_copy(
                 grad_query_ref.at[:, cols], grad_query_out.at[:, cols], store_semaphores.at[head]
             )
         )
         stores[-1].start()
+        for start in range(0, length, TILE):
+            key_part_ref[start : start + TILE, cols] = key_sums[start].T
+            value_part_ref[start : start + TILE, cols] = value_sums[start].T
     for store in stores:
         store.wait()
 
@@ -344,10 +354,10 @@
 ):
     low = state_ref[...].reshape(-1, HD).astype(BF16)
     stores = []
-    tails = turn(tail_rows(row_ref))
+    tails = tail_rows(row_ref)
     for head in range(key_ref.shape[1] // HD):
         cols = head_columns(head)
-        tail = tails[:, head : head + 1]
+        tail = down(cut(tails[head : head + 1]))
         grad_key_ref[:, cols] = (
             key_part_ref[:, cols] + tail * dot(value_ref[:, cols], low[cols], 1, 1)
         ).astype(BF16)
@@ -397,9 +407,9 @@
         ],
     )
     got = swap(first.reshape(blocks, rows + 1, 1, HD), "ctx").reshape(first.shape)
-    local, column, gain, turned = call(
+    local, gain, turned = call(
         local_kernel,
-        [like(whole), like((length, HD)), like((8, width)), like((width, length), BF16)],
+        [like(whole), like((8, width)), like((width, length), BF16)],
         queries,
         key_rows,
         values,
@@ -407,7 +417,7 @@
         gain,
         flops=2 * square,
         places_in={0: pltpu.HBM, 1: pltpu.HBM, 2: pltpu.HBM},
-        places_out={3: pltpu.HBM},
+        places_out={2: pltpu.HBM},
         scratch=[*three, pltpu.VMEM((width, length), BF16), pltpu.SemaphoreType.DMA],
     )
     states, totals = call(
@@ -422,7 +432,7 @@
         queries,
         local,
         state_in,
-        column,
+        row,
         grad_normed,
         gain,
         flops=narrow,
@@ -456,9 +466,14 @@
         low,
         row,
         flops=5 * square,
-        places_in={0: pltpu.HBM, 1: pltpu.HBM, 2: pltpu.HBM},
+        places_in={i: pltpu.HBM for i in range(4)},
         places_out={0: pltpu.HBM},
-        scratch=[*three, block, pltpu.SemaphoreType.DMA((heads,))],
+        scratch=[
+            *[block] * 4,
+            pltpu.SemaphoreType.DMA((4,)),
+            block,
+            pltpu.SemaphoreType.DMA((heads,)),
+        ],
     )
     grad_key, grad_value = call(
         finish_kernel,

time: 90.6 us -> 90.4 us (level)
  waiting for transfers between devices: 6.96 us -> 8.56 us
  local copies, waits for them, and re-layouts: 1.74 us -> 0.71 us
    all_to_all x2, waiting for transfers between devices: 6.96 us -> 8.56 us  [swap(): return lax.all_to_all(array, axis, 0, 0, tiled=True)]
    unnamed x16 -> x14, local copies, waits for them, and re-layouts: 1.74 us -> 0.71 us
  transfers between devices with their start and end apart: 2 -> 2, of which waited for: 2 -> 2; matrix products, arithmetic and copies ran while one was open for 0% -> 0% of each run, Pallas kernels for 11% -> 10%
where the time goes in v4:
time: 90.4 us; the launch traced here: 90 us
  blocking collectives  58 us (64%)
  Pallas kernels  14.6 us (16%)
  waiting for transfers between devices  8.56 us (9%)
  starting transfers between devices  7.39 us (8%)
    all_to_all x3, blocking collectives, swap(): return lax.all_to_all(array, axis, 0, 0, tiled=True)  58 us
    pallas_call x8, Pallas kernels, call(): pl.pallas_call(body, out_shape=[places_out[i](s.shape, s.dtype) if i in p...  14.6 us
    all_to_all x2, waiting for transfers between devices, swap(): return lax.all_to_all(array, axis, 0, 0, tiled=True)  8.56 us
    all_to_all x2, starting transfers between devices, swap(): return lax.all_to_all(array, axis, 0, 0, tiled=True)  7.39 us
  transfers between devices with their start and end apart: 2, of which 2 were waited for; matrix products, arithmetic and copies ran while one was open for 0% of the time, Pallas kernels for 10%

profile of v4, /device:TPU:1, one launch (start us, length us, event | category | flops | bytes accessed | tf_op | source)
XLA Modules:
  0.0 90.0 jit_solution(7995884943121247110)
XLA Ops:
  0.6 1.7 %shard_map.85 = (f32[544,128]{1,0:T(8,128)S(1)}, f32[8,512]{1,0:T(8,128)S(1)}) custom-call(f32[4,512]{1,0:T(4,128)} %log_in.1, bf16[512,512]{1,0:T(8,128)(2,1)} %key_ref.1, bf16[512,512]{1,0:T(8,128)(2,1)} %value_ref.1), custom_call_target="tpu_custom_call" | custom-call | flops 67108864 | bytes 1351680 | tf_op jit(solution)/shard_map/pallas_call | solution.py:36
  2.3 18.8 %all_to_all.25 = f32[32,17,1,128]{3,2,1,0:T(1,128)S(1)} all-to-all(f32[32,17,1,128]{3,2,1,0:T(1,128)S(1)} %bitcast.4), channel_id=1, replica_groups=mesh['ctx'=32,'head'=16] {'ctx'}, dimensions={0} | all-to-all | bytes 557056 | tf_op jit(solution)/shard_map/all_to_all | solution.py:388
  21.1 0.8 shard_map.87
  21.9 3.7 %all-to-all-start.1 = ((f32[32,16,128]{2,1,0:T(8,128)}), f32[32,16,128]{2,1,0:T(8,128)S(1)}, u32[]{:S(2)}, u32[]{:S(2)}) async-start(f32[32,16,128]{2,1,0:T(8,128)} %get-tuple-element.23), calls=%async_computation.1 | async-start | bytes 524288 | tf_op jit(solution)/shard_map/all_to_all | solution.py:388
  25.6 0.0 copy-start.6
  25.6 0.7 copy-done.6
  26.3 0.0 copy-start.2
  26.3 0.0 copy-start.3
  26.3 3.8 %shard_map.86 = (f32[512,512]{1,0:T(8,128)S(1)}, f32[8,512]{1,0:T(8,128)S(1)}, bf16[512,512]{1,0:T(8,128)(2,1)}) custom-call(bf16[512,512]{1,0:T(8,128)(2,1)} %query_in.3, bf16[512,512]{1,0:T(8,128)(2,1)} %key_ref.1, bf16[512,512]{1,0:T(8,128)(2,1)} %value_ref.1, f32[8,512]{1,0:T(8,128)S(1)} %get-tuple-element.20.row_ref, f32[1,512]{1,0:T(1,128)S(1)} %bitcast.5), custom_call_target="tpu_custom_call" | custom-call | flops 536870912 | bytes 3180544 | tf_op jit(solution)/shard_map/pallas_call | solution.py:36
  30.1 4.6 %all-to-all-done.1.state_ref = f32[32,16,128]{2,1,0:T(8,128)S(1)} async-done(((f32[32,16,128]{2,1,0:T(8,128)}), f32[32,16,128]{2,1,0:T(8,128)S(1)}, u32[]{:S(2)}, u32[]{:S(2)}) %all-to-all-start.1) | async-done | bytes 262176 | tf_op jit(solution)/shard_map/all_to_all | solution.py:388
  34.7 0.0 copy-done.2
  34.7 0.0 copy-done.3
  34.7 0.0 copy-start.4
  34.7 0.6 shard_map.88
  35.3 25.1 %all_to_all.26.sums_ref = f32[16,8,128]{2,1,0:T(8,128)S(1)} all-to-all(f32[16,8,128]{2,1,0:T(8,128)S(1)} %get-tuple-element.25), channel_id=1, replica_groups=mesh['ctx'=32,'head'=16] {'head'}, dimensions={0} | all-to-all | bytes 131072 | tf_op jit(solution)/shard_map/all_to_all | solution.py:388
  60.4 0.0 copy-done.4
  60.4 0.6 shard_map.89
  61.0 0.0 copy-start.5
  61.0 14.1 %all_to_all.27.got_ref = f32[32,16,128]{2,1,0:T(8,128)S(1)} all-to-all(f32[32,16,128]{2,1,0:T(8,128)S(1)} %get-tuple-element.33), channel_id=1, replica_groups=mesh['ctx'=32,'head'=16] {'ctx'}, dimensions={0} | all-to-all | bytes 524288 | tf_op jit(solution)/shard_map/all_to_all | solution.py:388
  75.1 0.8 shard_map.91
  75.9 0.0 copy-done.5
  75.9 3.7 %all-to-all-start.4 = ((f32[32,16,128]{2,1,0:T(8,128)}), f32[32,16,128]{2,1,0:T(8,128)S(1)}, u32[]{:S(2)}, u32[]{:S(2)}) async-start(f32[32,16,128]{2,1,0:T(8,128)} %shard_map.91), calls=%async_computation.4 | async-start | bytes 524288 | tf_op jit(solution)/shard_map/all_to_all | solution.py:388
  79.6 0.0 copy-start
  79.6 0.0 copy-start.1
  79.6 5.1 %shard_map.90 = (bf16[512,512]{1,0:T(8,128)(2,1)}, f32[512,512]{1,0:T(8,128)S(1)}, f32[512,512]{1,0:T(8,128)S(1)}) custom-call(bf16[512,512]{1,0:T(8,128)(2,1)} %query_in.3, bf16[512,512]{1,0:T(8,128)(2,1)} %key_ref.1, bf16[512,512]{1,0:T(8,128)(2,1)} %value_ref.1, bf16[512,512]{1,0:T(8,128)(2,1)} %copy-done.5, ...), custom_call_target="tpu_custom_call" | custom-call | flops 1342177280 | bytes 4866048 | tf_op jit(solution)/shard_map/pallas_call | solution.py:36
  84.7 4.0 %all-to-all-done.4.state_ref = f32[32,16,128]{2,1,0:T(8,128)S(1)} async-done(((f32[32,16,128]{2,1,0:T(8,128)}), f32[32,16,128]{2,1,0:T(8,128)S(1)}, u32[]{:S(2)}, u32[]{:S(2)}) %all-to-all-start.4) | async-done | bytes 262176 | tf_op jit(solution)/shard_map/all_to_all | solution.py:388
  88.7 0.0 copy-done
  88.7 0.0 copy-done.1
  88.7 1.3 %shard_map.92 = (bf16[512,512]{1,0:T(8,128)(2,1)}, bf16[512,512]{1,0:T(8,128)(2,1)}) custom-call(f32[512,512]{1,0:T(8,128)S(1)} %get-tuple-element.31.key_part_ref, f32[512,512]{1,0:T(8,128)S(1)} %get-tuple-element.32.value_part_ref, bf16[512,512]{1,0:T(8,128)(2,1)S(1)} %copy-done, bf16[512,512]{1,0:T(8,128)(2,1)S(1)} %copy-done.1, ...), custom_call_target="tpu_custom_call" | custom-call | flops 134217728 | bytes 4472832 | tf_op jit(solution)/shard_map/pallas_call | solution.py:36
Async XLA Ops:
  21.9 12.8 %all-to-all-start.1 = ((f32[32,16,128]{2,1,0:T(8,128)}), f32[32,16,128]{2,1,0:T(8,128)S(1)}, u32[]{:S(2)}, u32[]{:S(2)}) async-start(f32[32,16,128]{2,1,0:T(8,128)} %get-tuple-element.23), calls=%async_computation.1 | async-start | bytes 524288 | tf_op jit(solution)/shard_map/all_to_all | solution.py:388
  25.6 0.7 copy-start.6
  26.3 8.4 %copy-start.2 = (bf16[512,512]{1,0:T(8,128)(2,1)S(1)}, bf16[512,512]{1,0:T(8,128)(2,1)}, u32[]{:S(2)}) copy-start(bf16[512,512]{1,0:T(8,128)(2,1)} %normed_ref.3) | copy-start | bytes 1572868
  26.3 8.4 %copy-start.3 = (bf16[512,512]{1,0:T(8,128)(2,1)S(1)}, bf16[512,512]{1,0:T(8,128)(2,1)}, u32[]{:S(2)}) copy-start(bf16[512,512]{1,0:T(8,128)(2,1)} %query_in.3) | copy-start | bytes 1572868
  34.7 25.7 %copy-start.4 = (bf16[512,512]{1,0:T(8,128)(2,1)S(1)}, bf16[512,512]{1,0:T(8,128)(2,1)}, u32[]{:S(2)}) copy-start(bf16[512,512]{1,0:T(8,128)(2,1)} %get-tuple-element.27.turned_ref) | copy-start | bytes 1572868
  61.0 14.9 %copy-start.5 = (bf16[512,512]{1,0:T(8,128)(2,1)}, bf16[512,512]{1,0:T(8,128)(2,1)S(1)}, u32[]{:S(2)}) copy-start(bf16[512,512]{1,0:T(8,128)(2,1)S(1)} %get-tuple-element.28.grad_in) | copy-start | bytes 1572868
  75.9 12.8 %all-to-all-start.4 = ((f32[32,16,128]{2,1,0:T(8,128)}), f32[32,16,128]{2,1,0:T(8,128)S(1)}, u32[]{:S(2)}, u32[]{:S(2)}) async-start(f32[32,16,128]{2,1,0:T(8,128)} %shard_map.91), calls=%async_computation.4 | async-start | bytes 524288 | tf_op jit(solution)/shard_map/all_to_all | solution.py:388
  79.6 9.1 %copy-start = (bf16[512,512]{1,0:T(8,128)(2,1)S(1)}, bf16[512,512]{1,0:T(8,128)(2,1)}, u32[]{:S(2)}) copy-start(bf16[512,512]{1,0:T(8,128)(2,1)} %key_ref.1) | copy-start | bytes 1572868
  79.6 9.1 %copy-start.1 = (bf16[512,512]{1,0:T(8,128)(2,1)S(1)}, bf16[512,512]{1,0:T(8,128)(2,1)}, u32[]{:S(2)}) copy-start(bf16[512,512]{1,0:T(8,128)(2,1)} %value_ref.1) | copy-start | bytes 1572868

commit v5 on v4

--- a/solution.py
+++ b/solution.py
@@ -147,10 +147,20 @@
             send_ref[first : first + rows] = update[i * rows : (i + 1) * rows]
 
 
-def forward_kernel(got_ref, send_ref, total_ref):
-    blocks, rows = send_ref.shape[:2]
+def exchange_order(blocks):
+    if blocks != 32:
+        return tuple(reversed(range(blocks)))
+    order = []
+    for block in reversed(range(0, blocks, 2)):
+        x, y, core = block // 8, block // 2 % 4, block % 2
+        order += [((x + 2) % 4 * 4 + (y + 2) % 4) * 2 + 1 - core, block]
+    return tuple(order)
+
+
+def forward_kernel(order, got_ref, send_ref, total_ref):
+    rows = send_ref.shape[1]
     state = jnp.zeros((rows, HD), F32)
-    for block in range(blocks):
+    for block in (order.index(i) for i in range(len(order))):
         first = block * (rows + 1)
         send_ref[block] = state
         total = got_ref[first + rows : first + rows + 1]
@@ -158,11 +168,11 @@
         state = jnp.exp(total) * state + got_ref[first : first + rows]
 
 
-def backward_kernel(got_ref, total_ref, send_ref):
-    blocks, rows = send_ref.shape[:2]
+def backward_kernel(order, got_ref, total_ref, send_ref):
+    rows = send_ref.shape[1]
     factors = jnp.exp(total_ref[:, :1, :])
     state = jnp.zeros((rows, HD), F32)
-    for block in reversed(range(blocks)):
+    for block in (order.index(i) for i in reversed(range(len(order)))):
         send_ref[block] = state
         state = factors[block] * state + got_ref[block]
 
@@ -384,8 +394,11 @@
     square = 2 * length * length * HD * heads
     narrow = 2 * length * HD * HD * heads
 
+    order = exchange_order(blocks)
+
     def swap(array, axis):
-        return lax.all_to_all(array, axis, 0, 0, tiled=True)
+        groups = [list(order)] if axis == "ctx" else None
+        return lax.all_to_all(array, axis, 0, 0, axis_index_groups=groups, tiled=True)
 
     whole = (length, width)
     block = pltpu.VMEM(whole, BF16)
@@ -421,7 +434,7 @@
         scratch=[*three, pltpu.VMEM((width, length), BF16), pltpu.SemaphoreType.DMA],
     )
     states, totals = call(
-        forward_kernel,
+        functools.partial(forward_kernel, order),
         [like((blocks, rows, HD)), like((blocks, 8, HD))],
         got,
     )
@@ -450,7 +463,7 @@
     )
     got = swap(second, "ctx")
     (states,) = call(
-        backward_kernel,
+        functools.partial(backward_kernel, order),
         [like((blocks, rows, HD))],
         got,
         totals,

time: 90.4 us -> 87.5 us (0.968)
  waiting for transfers between devices: 8.56 us -> 4.96 us
  starting transfers between devices: 7.39 us -> 10.8 us
  blocking collectives: 58 us -> 55.2 us
    all_to_all x2, waiting for transfers between devices: 8.56 us -> 4.96 us  [swap(): lax.all_to_all(array, axis, 0, 0, axis_index_groups=groups, tiled=True)]
    all_to_all x2, starting transfers between devices: 7.39 us -> 10.8 us  [swap(): lax.all_to_all(array, axis, 0, 0, axis_index_groups=groups, tiled=True)]
    all_to_all x3, blocking collectives: 58 us -> 55.2 us  [swap(): lax.all_to_all(array, axis, 0, 0, axis_index_groups=groups, tiled=True)]
where the time goes in v5:
time: 87.5 us; the launch traced here: 87 us
  blocking collectives  55.2 us (63%)
  Pallas kernels  14.6 us (17%)
  starting transfers between devices  10.8 us (12%)
  waiting for transfers between devices  4.96 us (6%)
    all_to_all x3, blocking collectives, swap(): lax.all_to_all(array, axis, 0, 0, axis_index_groups=groups, tiled=True)  55.2 us
    pallas_call x8, Pallas kernels, call(): pl.pallas_call(body, out_shape=[places_out[i](s.shape, s.dtype) if i in p...  14.6 us
    all_to_all x2, starting transfers between devices, swap(): lax.all_to_all(array, axis, 0, 0, axis_index_groups=groups, tiled=True)  10.8 us
    all_to_all x2, waiting for transfers between devices, swap(): lax.all_to_all(array, axis, 0, 0, axis_index_groups=groups, tiled=True)  4.96 us
  transfers between devices with their start and end apart: 2, of which 2 were waited for; matrix products, arithmetic and copies ran while one was open for 0% of the time, Pallas kernels for 10%

profile of v5, /device:TPU:1, one launch (start us, length us, event | category | flops | bytes accessed | tf_op | source)
XLA Modules:
  0.0 87.0 jit_solution(18332939853318486852)
XLA Ops:
  0.6 1.7 %shard_map.85 = (f32[544,128]{1,0:T(8,128)S(1)}, f32[8,512]{1,0:T(8,128)S(1)}) custom-call(f32[4,512]{1,0:T(4,128)} %log_in.1, bf16[512,512]{1,0:T(8,128)(2,1)} %key_ref.1, bf16[512,512]{1,0:T(8,128)(2,1)} %value_ref.1), custom_call_target="tpu_custom_call" | custom-call | flops 67108864 | bytes 1351680 | tf_op jit(solution)/shard_map/pallas_call | solution.py:36
  2.3 17.7 %all_to_all.25 = f32[32,17,1,128]{3,2,1,0:T(1,128)S(1)} all-to-all(f32[32,17,1,128]{3,2,1,0:T(1,128)S(1)} %bitcast.4), channel_id=1, replica_groups={{176,480,144,448,240,416,208,384,48,352,16,320,112,288,80,256,432,224,4..., dimensions={0} | all-to-all | bytes 557056 | tf_op jit(solution)/shard_map/all_to_all | solution.py:401
  20.0 0.8 shard_map.87
  20.8 5.4 %all-to-all-start.1 = ((f32[32,16,128]{2,1,0:T(8,128)}), f32[32,16,128]{2,1,0:T(8,128)S(1)}, u32[]{:S(2)}, u32[]{:S(2)}) async-start(f32[32,16,128]{2,1,0:T(8,128)} %get-tuple-element.23), calls=%async_computation.1 | async-start | bytes 524288 | tf_op jit(solution)/shard_map/all_to_all | solution.py:401
  26.2 0.0 copy-start.6
  26.2 0.7 copy-done.6
  26.9 0.0 copy-start.2
  26.9 0.0 copy-start.3
  26.9 3.8 %shard_map.86 = (f32[512,512]{1,0:T(8,128)S(1)}, f32[8,512]{1,0:T(8,128)S(1)}, bf16[512,512]{1,0:T(8,128)(2,1)}) custom-call(bf16[512,512]{1,0:T(8,128)(2,1)} %query_in.3, bf16[512,512]{1,0:T(8,128)(2,1)} %key_ref.1, bf16[512,512]{1,0:T(8,128)(2,1)} %value_ref.1, f32[8,512]{1,0:T(8,128)S(1)} %get-tuple-element.20.row_ref, f32[1,512]{1,0:T(1,128)S(1)} %bitcast.5), custom_call_target="tpu_custom_call" | custom-call | flops 536870912 | bytes 3180544 | tf_op jit(solution)/shard_map/pallas_call | solution.py:36
  30.7 2.8 %all-to-all-done.1.state_ref = f32[32,16,128]{2,1,0:T(8,128)S(1)} async-done(((f32[32,16,128]{2,1,0:T(8,128)}), f32[32,16,128]{2,1,0:T(8,128)S(1)}, u32[]{:S(2)}, u32[]{:S(2)}) %all-to-all-start.1) | async-done | bytes 262176 | tf_op jit(solution)/shard_map/all_to_all | solution.py:401
  33.5 0.0 copy-done.2
  33.5 0.0 copy-done.3
  33.5 0.0 copy-start.4
  33.5 0.6 shard_map.88
  34.1 24.4 %all_to_all.26.sums_ref = f32[16,8,128]{2,1,0:T(8,128)S(1)} all-to-all(f32[16,8,128]{2,1,0:T(8,128)S(1)} %get-tuple-element.25), channel_id=1, replica_groups=mesh['ctx'=32,'head'=16] {'head'}, dimensions={0} | all-to-all | bytes 131072 | tf_op jit(solution)/shard_map/all_to_all | solution.py:401
  58.5 0.0 copy-done.4
  58.5 0.6 shard_map.89
  59.1 0.0 copy-start.5
  59.1 13.2 %all_to_all.27.got_ref = f32[32,16,128]{2,1,0:T(8,128)S(1)} all-to-all(f32[32,16,128]{2,1,0:T(8,128)S(1)} %get-tuple-element.33), channel_id=1, replica_groups={{176,480,144,448,240,416,208,384,48,352,16,320,112,288,80,256,432,224,4..., dimensions={0} | all-to-all | bytes 524288 | tf_op jit(solution)/shard_map/all_to_all | solution.py:401
  72.3 0.8 shard_map.91
  73.1 0.0 copy-done.5
  73.1 5.4 %all-to-all-start.4 = ((f32[32,16,128]{2,1,0:T(8,128)}), f32[32,16,128]{2,1,0:T(8,128)S(1)}, u32[]{:S(2)}, u32[]{:S(2)}) async-start(f32[32,16,128]{2,1,0:T(8,128)} %shard_map.91), calls=%async_computation.4 | async-start | bytes 524288 | tf_op jit(solution)/shard_map/all_to_all | solution.py:401
  78.5 0.0 copy-start
  78.5 0.0 copy-start.1
  78.5 5.1 %shard_map.90 = (bf16[512,512]{1,0:T(8,128)(2,1)}, f32[512,512]{1,0:T(8,128)S(1)}, f32[512,512]{1,0:T(8,128)S(1)}) custom-call(bf16[512,512]{1,0:T(8,128)(2,1)} %query_in.3, bf16[512,512]{1,0:T(8,128)(2,1)} %key_ref.1, bf16[512,512]{1,0:T(8,128)(2,1)} %value_ref.1, bf16[512,512]{1,0:T(8,128)(2,1)} %copy-done.5, ...), custom_call_target="tpu_custom_call" | custom-call | flops 1342177280 | bytes 4866048 | tf_op jit(solution)/shard_map/pallas_call | solution.py:36
  83.6 2.2 %all-to-all-done.4.state_ref = f32[32,16,128]{2,1,0:T(8,128)S(1)} async-done(((f32[32,16,128]{2,1,0:T(8,128)}), f32[32,16,128]{2,1,0:T(8,128)S(1)}, u32[]{:S(2)}, u32[]{:S(2)}) %all-to-all-start.4) | async-done | bytes 262176 | tf_op jit(solution)/shard_map/all_to_all | solution.py:401
  85.8 0.0 copy-done
  85.8 0.0 copy-done.1
  85.8 1.3 %shard_map.92 = (bf16[512,512]{1,0:T(8,128)(2,1)}, bf16[512,512]{1,0:T(8,128)(2,1)}) custom-call(f32[512,512]{1,0:T(8,128)S(1)} %get-tuple-element.31.key_part_ref, f32[512,512]{1,0:T(8,128)S(1)} %get-tuple-element.32.value_part_ref, bf16[512,512]{1,0:T(8,128)(2,1)S(1)} %copy-done, bf16[512,512]{1,0:T(8,128)(2,1)S(1)} %copy-done.1, ...), custom_call_target="tpu_custom_call" | custom-call | flops 134217728 | bytes 4472832 | tf_op jit(solution)/shard_map/pallas_call | solution.py:36
Async XLA Ops:
  20.8 12.8 %all-to-all-start.1 = ((f32[32,16,128]{2,1,0:T(8,128)}), f32[32,16,128]{2,1,0:T(8,128)S(1)}, u32[]{:S(2)}, u32[]{:S(2)}) async-start(f32[32,16,128]{2,1,0:T(8,128)} %get-tuple-element.23), calls=%async_computation.1 | async-start | bytes 524288 | tf_op jit(solution)/shard_map/all_to_all | solution.py:401
  26.2 0.7 copy-start.6
  26.9 6.6 %copy-start.2 = (bf16[512,512]{1,0:T(8,128)(2,1)S(1)}, bf16[512,512]{1,0:T(8,128)(2,1)}, u32[]{:S(2)}) copy-start(bf16[512,512]{1,0:T(8,128)(2,1)} %normed_ref.3) | copy-start | bytes 1572868
  26.9 6.6 %copy-start.3 = (bf16[512,512]{1,0:T(8,128)(2,1)S(1)}, bf16[512,512]{1,0:T(8,128)(2,1)}, u32[]{:S(2)}) copy-start(bf16[512,512]{1,0:T(8,128)(2,1)} %query_in.3) | copy-start | bytes 1572868
  33.5 25.0 %copy-start.4 = (bf16[512,512]{1,0:T(8,128)(2,1)S(1)}, bf16[512,512]{1,0:T(8,128)(2,1)}, u32[]{:S(2)}) copy-start(bf16[512,512]{1,0:T(8,128)(2,1)} %get-tuple-element.27.turned_ref) | copy-start | bytes 1572868
  59.1 14.0 %copy-start.5 = (bf16[512,512]{1,0:T(8,128)(2,1)}, bf16[512,512]{1,0:T(8,128)(2,1)S(1)}, u32[]{:S(2)}) copy-start(bf16[512,512]{1,0:T(8,128)(2,1)S(1)} %get-tuple-element.28.grad_in) | copy-start | bytes 1572868
  73.1 12.7 %all-to-all-start.4 = ((f32[32,16,128]{2,1,0:T(8,128)}), f32[32,16,128]{2,1,0:T(8,128)S(1)}, u32[]{:S(2)}, u32[]{:S(2)}) async-start(f32[32,16,128]{2,1,0:T(8,128)} %shard_map.91), calls=%async_computation.4 | async-start | bytes 524288 | tf_op jit(solution)/shard_map/all_to_all | solution.py:401
  78.5 7.3 %copy-start = (bf16[512,512]{1,0:T(8,128)(2,1)S(1)}, bf16[512,512]{1,0:T(8,128)(2,1)}, u32[]{:S(2)}) copy-start(bf16[512,512]{1,0:T(8,128)(2,1)} %key_ref.1) | copy-start | bytes 1572868
  78.5 7.3 %copy-start.1 = (bf16[512,512]{1,0:T(8,128)(2,1)S(1)}, bf16[512,512]{1,0:T(8,128)(2,1)}, u32[]{:S(2)}) copy-start(bf16[512,512]{1,0:T(8,128)(2,1)} %value_ref.1) | copy-start | bytes 1572868

commit v6 on v5

--- a/solution.py
+++ b/solution.py
@@ -397,8 +397,8 @@
     order = exchange_order(blocks)
 
     def swap(array, axis):
-        groups = [list(order)] if axis == "ctx" else None
-        return lax.all_to_all(array, axis, 0, 0, axis_index_groups=groups, tiled=True)
+        members = list(order) if axis == "ctx" else [7 * i % groups for i in range(groups)][::-1]
+        return lax.all_to_all(array, axis, 0, 0, axis_index_groups=[members], tiled=True)
 
     whole = (length, width)
     block = pltpu.VMEM(whole, BF16)

time: 87.5 us -> 82.1 us (0.938)
  blocking collectives: 55.2 us -> 49.8 us
    all_to_all x3, blocking collectives: 55.2 us -> 49.8 us  [swap(): lax.all_to_all(array, axis, 0, 0, axis_index_groups=[members], tiled=True)]
  transfers between devices with their start and end apart: 2 -> 2, of which waited for: 2 -> 2; matrix products, arithmetic and copies ran while one was open for 0% -> 0% of each run, Pallas kernels for 10% -> 11%
where the time goes in v6:
time: 82.1 us; the launch traced here: 81.6 us
  blocking collectives  49.8 us (61%)
  Pallas kernels  14.6 us (18%)
  starting transfers between devices  10.8 us (13%)
  waiting for transfers between devices  4.96 us (6%)
    all_to_all x3, blocking collectives, swap(): lax.all_to_all(array, axis, 0, 0, axis_index_groups=[members], tiled=True)  49.8 us
    pallas_call x8, Pallas kernels, call(): pl.pallas_call(body, out_shape=[places_out[i](s.shape, s.dtype) if i in p...  14.6 us
    all_to_all x2, starting transfers between devices, swap(): lax.all_to_all(array, axis, 0, 0, axis_index_groups=[members], tiled=True)  10.8 us
    all_to_all x2, waiting for transfers between devices, swap(): lax.all_to_all(array, axis, 0, 0, axis_index_groups=[members], tiled=True)  4.96 us
  transfers between devices with their start and end apart: 2, of which 2 were waited for; matrix products, arithmetic and copies ran while one was open for 0% of the time, Pallas kernels for 11%

profile of v6, /device:TPU:1, one launch (start us, length us, event | category | flops | bytes accessed | tf_op | source)
XLA Modules:
  0.0 81.6 jit_solution(17642127130329512384)
XLA Ops:
  0.6 1.7 %shard_map.85 = (f32[544,128]{1,0:T(8,128)S(1)}, f32[8,512]{1,0:T(8,128)S(1)}) custom-call(f32[4,512]{1,0:T(4,128)} %log_in.1, bf16[512,512]{1,0:T(8,128)(2,1)} %key_ref.1, bf16[512,512]{1,0:T(8,128)(2,1)} %value_ref.1), custom_call_target="tpu_custom_call" | custom-call | flops 67108864 | bytes 1351680 | tf_op jit(solution)/shard_map/pallas_call | solution.py:36
  2.3 17.7 %all_to_all.25 = f32[32,17,1,128]{3,2,1,0:T(1,128)S(1)} all-to-all(f32[32,17,1,128]{3,2,1,0:T(1,128)S(1)} %bitcast.4), channel_id=1, replica_groups={{176,480,144,448,240,416,208,384,48,352,16,320,112,288,80,256,432,224,4..., dimensions={0} | all-to-all | bytes 557056 | tf_op jit(solution)/shard_map/all_to_all | solution.py:401
  20.0 0.8 shard_map.87
  20.8 5.4 %all-to-all-start.1 = ((f32[32,16,128]{2,1,0:T(8,128)}), f32[32,16,128]{2,1,0:T(8,128)S(1)}, u32[]{:S(2)}, u32[]{:S(2)}) async-start(f32[32,16,128]{2,1,0:T(8,128)} %get-tuple-element.23), calls=%async_computation.1 | async-start | bytes 524288 | tf_op jit(solution)/shard_map/all_to_all | solution.py:401
  26.2 0.0 copy-start.6
  26.2 0.7 copy-done.6
  26.9 0.0 copy-start.2
  26.9 0.0 copy-start.3
  26.9 3.8 %shard_map.86 = (f32[512,512]{1,0:T(8,128)S(1)}, f32[8,512]{1,0:T(8,128)S(1)}, bf16[512,512]{1,0:T(8,128)(2,1)}) custom-call(bf16[512,512]{1,0:T(8,128)(2,1)} %query_in.3, bf16[512,512]{1,0:T(8,128)(2,1)} %key_ref.1, bf16[512,512]{1,0:T(8,128)(2,1)} %value_ref.1, f32[8,512]{1,0:T(8,128)S(1)} %get-tuple-element.20.row_ref, f32[1,512]{1,0:T(1,128)S(1)} %bitcast.5), custom_call_target="tpu_custom_call" | custom-call | flops 536870912 | bytes 3180544 | tf_op jit(solution)/shard_map/pallas_call | solution.py:36
  30.7 2.8 %all-to-all-done.1.state_ref = f32[32,16,128]{2,1,0:T(8,128)S(1)} async-done(((f32[32,16,128]{2,1,0:T(8,128)}), f32[32,16,128]{2,1,0:T(8,128)S(1)}, u32[]{:S(2)}, u32[]{:S(2)}) %all-to-all-start.1) | async-done | bytes 262176 | tf_op jit(solution)/shard_map/all_to_all | solution.py:401
  33.5 0.0 copy-done.2
  33.5 0.0 copy-done.3
  33.5 0.0 copy-start.4
  33.5 0.6 shard_map.88
  34.1 19.3 %all_to_all.26.sums_ref = f32[16,8,128]{2,1,0:T(8,128)S(1)} all-to-all(f32[16,8,128]{2,1,0:T(8,128)S(1)} %get-tuple-element.25), channel_id=1, replica_groups={{9,2,11,4,13,6,15,8,1,10,3,12,5,14,7,0},{25,18,27,20,29,22,31,24,17,26,..., dimensions={0} | all-to-all | bytes 131072 | tf_op jit(solution)/shard_map/all_to_all | solution.py:401
  53.4 0.0 copy-done.4
  53.4 0.6 shard_map.89
  54.0 0.0 copy-start.5
  54.0 12.9 %all_to_all.27.got_ref = f32[32,16,128]{2,1,0:T(8,128)S(1)} all-to-all(f32[32,16,128]{2,1,0:T(8,128)S(1)} %get-tuple-element.33), channel_id=1, replica_groups={{176,480,144,448,240,416,208,384,48,352,16,320,112,288,80,256,432,224,4..., dimensions={0} | all-to-all | bytes 524288 | tf_op jit(solution)/shard_map/all_to_all | solution.py:401
  66.9 0.8 shard_map.91
  67.7 0.0 copy-done.5
  67.7 5.4 %all-to-all-start.4 = ((f32[32,16,128]{2,1,0:T(8,128)}), f32[32,16,128]{2,1,0:T(8,128)S(1)}, u32[]{:S(2)}, u32[]{:S(2)}) async-start(f32[32,16,128]{2,1,0:T(8,128)} %shard_map.91), calls=%async_computation.4 | async-start | bytes 524288 | tf_op jit(solution)/shard_map/all_to_all | solution.py:401
  73.1 0.0 copy-start
  73.1 0.0 copy-start.1
  73.1 5.1 %shard_map.90 = (bf16[512,512]{1,0:T(8,128)(2,1)}, f32[512,512]{1,0:T(8,128)S(1)}, f32[512,512]{1,0:T(8,128)S(1)}) custom-call(bf16[512,512]{1,0:T(8,128)(2,1)} %query_in.3, bf16[512,512]{1,0:T(8,128)(2,1)} %key_ref.1, bf16[512,512]{1,0:T(8,128)(2,1)} %value_ref.1, bf16[512,512]{1,0:T(8,128)(2,1)} %copy-done.5, ...), custom_call_target="tpu_custom_call" | custom-call | flops 1342177280 | bytes 4866048 | tf_op jit(solution)/shard_map/pallas_call | solution.py:36
  78.2 2.2 %all-to-all-done.4.state_ref = f32[32,16,128]{2,1,0:T(8,128)S(1)} async-done(((f32[32,16,128]{2,1,0:T(8,128)}), f32[32,16,128]{2,1,0:T(8,128)S(1)}, u32[]{:S(2)}, u32[]{:S(2)}) %all-to-all-start.4) | async-done | bytes 262176 | tf_op jit(solution)/shard_map/all_to_all | solution.py:401
  80.4 0.0 copy-done
  80.4 0.0 copy-done.1
  80.4 1.3 %shard_map.92 = (bf16[512,512]{1,0:T(8,128)(2,1)}, bf16[512,512]{1,0:T(8,128)(2,1)}) custom-call(f32[512,512]{1,0:T(8,128)S(1)} %get-tuple-element.31.key_part_ref, f32[512,512]{1,0:T(8,128)S(1)} %get-tuple-element.32.value_part_ref, bf16[512,512]{1,0:T(8,128)(2,1)S(1)} %copy-done, bf16[512,512]{1,0:T(8,128)(2,1)S(1)} %copy-done.1, ...), custom_call_target="tpu_custom_call" | custom-call | flops 134217728 | bytes 4472832 | tf_op jit(solution)/shard_map/pallas_call | solution.py:36
Async XLA Ops:
  20.8 12.8 %all-to-all-start.1 = ((f32[32,16,128]{2,1,0:T(8,128)}), f32[32,16,128]{2,1,0:T(8,128)S(1)}, u32[]{:S(2)}, u32[]{:S(2)}) async-start(f32[32,16,128]{2,1,0:T(8,128)} %get-tuple-element.23), calls=%async_computation.1 | async-start | bytes 524288 | tf_op jit(solution)/shard_map/all_to_all | solution.py:401
  26.2 0.7 copy-start.6
  26.9 6.6 %copy-start.2 = (bf16[512,512]{1,0:T(8,128)(2,1)S(1)}, bf16[512,512]{1,0:T(8,128)(2,1)}, u32[]{:S(2)}) copy-start(bf16[512,512]{1,0:T(8,128)(2,1)} %normed_ref.3) | copy-start | bytes 1572868
  26.9 6.6 %copy-start.3 = (bf16[512,512]{1,0:T(8,128)(2,1)S(1)}, bf16[512,512]{1,0:T(8,128)(2,1)}, u32[]{:S(2)}) copy-start(bf16[512,512]{1,0:T(8,128)(2,1)} %query_in.3) | copy-start | bytes 1572868
  33.5 19.9 %copy-start.4 = (bf16[512,512]{1,0:T(8,128)(2,1)S(1)}, bf16[512,512]{1,0:T(8,128)(2,1)}, u32[]{:S(2)}) copy-start(bf16[512,512]{1,0:T(8,128)(2,1)} %get-tuple-element.27.turned_ref) | copy-start | bytes 1572868
  54.0 13.7 %copy-start.5 = (bf16[512,512]{1,0:T(8,128)(2,1)}, bf16[512,512]{1,0:T(8,128)(2,1)S(1)}, u32[]{:S(2)}) copy-start(bf16[512,512]{1,0:T(8,128)(2,1)S(1)} %get-tuple-element.28.grad_in) | copy-start | bytes 1572868
  67.7 12.7 %all-to-all-start.4 = ((f32[32,16,128]{2,1,0:T(8,128)}), f32[32,16,128]{2,1,0:T(8,128)S(1)}, u32[]{:S(2)}, u32[]{:S(2)}) async-start(f32[32,16,128]{2,1,0:T(8,128)} %shard_map.91), calls=%async_computation.4 | async-start | bytes 524288 | tf_op jit(solution)/shard_map/all_to_all | solution.py:401
  73.1 7.3 %copy-start = (bf16[512,512]{1,0:T(8,128)(2,1)S(1)}, bf16[512,512]{1,0:T(8,128)(2,1)}, u32[]{:S(2)}) copy-start(bf16[512,512]{1,0:T(8,128)(2,1)} %key_ref.1) | copy-start | bytes 1572868
  73.1 7.3 %copy-start.1 = (bf16[512,512]{1,0:T(8,128)(2,1)S(1)}, bf16[512,512]{1,0:T(8,128)(2,1)}, u32[]{:S(2)}) copy-start(bf16[512,512]{1,0:T(8,128)(2,1)} %value_ref.1) | copy-start | bytes 1572868
